TPU v7x, 128 devices: a whole 4x4x4 slice. The times are simulated.
128 devices in a mesh: seq: 32 (over y, z_lo, x), ffn: 4 (over z_hi, core).
Axes of the slice: x: 4, y: 4, z: 4 (z_hi: 2, z_lo: 2; z = z_hi * 2 + z_lo), core: 2. Of those that a mesh axis runs over, the one named last changes fastest.
Arguments:
- tokens: bfloat16 [8192, 1024], P('seq'), may hold values from -6 to 6
- segment_kind: int32 [8192], P('seq'), may hold values from 0 to 2
- document: int32 [8192], replicated, may hold values from 0 to 3, as said below
- type_table: bfloat16 [3, 1024], replicated, may hold values from -3 to 3
- attend_gain: bfloat16 [1024], replicated, may hold values from 0.25 to 1.75
- attend_bias: bfloat16 [1024], replicated, may hold values from -1.75 to 1.75
- input_weight: bfloat16 [3, 1024, 1024], P(None, None, 'ffn')
- input_bias: bfloat16 [3, 1024], P(None, 'ffn'), may hold values from -1.75 to 1.75
- inner_gain: bfloat16 [1024], P('ffn'), may hold values from 0.25 to 1.75
- inner_bias: bfloat16 [1024], P('ffn'), may hold values from -1.75 to 1.75
- output_weight: bfloat16 [1024, 1024], P('ffn'), may hold values from -0.1875 to 0.1875
- output_bias: bfloat16 [1024], replicated, may hold values from -1.75 to 1.75
- feed_gain: bfloat16 [1024], replicated, may hold values from 0.25 to 1.75
- feed_bias: bfloat16 [1024], replicated, may hold values from -1.75 to 1.75
- up_weight: bfloat16 [1024, 4096], P(None, 'ffn')
- up_bias: bfloat16 [4096], P('ffn'), may hold values from -1.75 to 1.75
- hidden_gain: bfloat16 [4096], P('ffn'), may hold values from 0.25 to 1.75
- hidden_bias: bfloat16 [4096], P('ffn'), may hold values from -1.75 to 1.75
- down_weight: bfloat16 [4096, 1024], P('ffn'), may hold values from -0.09375 to 0.09375
- down_bias: bfloat16 [1024], replicated, may hold values from -1.75 to 1.75
- cotangent: bfloat16 [8192, 1024], P('seq'), may hold values from -6 to 6
Outputs:
- result: bfloat16 [8192, 1024], P('seq')
- grad_tokens: float32 [8192, 1024], P('seq')
- grad_type_table: float32 [3, 1024], replicated
- grad_attend_gain: float32 [1024], replicated
- grad_attend_bias: float32 [1024], replicated
- grad_input_weight: float32 [3, 1024, 1024], P(None, None, 'ffn')
- grad_input_bias: float32 [3, 1024], P(None, 'ffn')
- grad_inner_gain: float32 [1024], P('ffn')
- grad_inner_bias: float32 [1024], P('ffn')
- grad_output_weight: float32 [1024, 1024], P('ffn')
- grad_output_bias: float32 [1024], replicated
- grad_feed_gain: float32 [1024], replicated
- grad_feed_bias: float32 [1024], replicated
- grad_up_weight: float32 [1024, 4096], P(None, 'ffn')
- grad_up_bias: float32 [4096], P('ffn')
- grad_hidden_gain: float32 [4096], P('ffn')
- grad_hidden_bias: float32 [4096], P('ffn')
- grad_down_weight: float32 [4096, 1024], P('ffn')
- grad_down_bias: float32 [1024], replicated
Inputs may be any that keep to these rules, and one draw needn't show every extreme that they name: `document`: document numbers start at 0 and rise by 0 or 1 from one token to the next.
All inputs are finite; a program needn't handle non-finite values.
Results may differ from a plain program's by a relative error of at most 0.0095.
Values may be sent and summed in bfloat16 or wider, within the bound.
No kernel may reach another device: no remote copies, remote signals or barrier semaphores. Data moves between devices by JAX's collectives and lax.ppermute only.
A program may use at most 128 MiB of HBM per device.

v0:
```python
from functools import partial
import math

import jax
import jax.numpy as jnp
from jax import lax
from jax.sharding import PartitionSpec as P

D = 1024
FF = 4096
HEAD_DIM = 64


epsilon = 1e-05
scale_base = 512.0
masked_score = -1e30
highest = lax.Precision.HIGHEST


def xpos_tables(positions, head_width, total_rows):
    half_width = head_width // 2
    pair_index = jnp.arange(half_width, dtype=jnp.float32)
    frequency = 1.0 / 10000.0 ** (pair_index / half_width)
    angles = positions.astype(jnp.float32)[:, None] * frequency[None, :]
    ratios = (2.0 * pair_index + 0.4 * head_width) / (1.4 * head_width)
    exponent = (positions - total_rows // 2).astype(jnp.float32)[:, None] / scale_base
    growth = ratios[None, :] ** exponent
    return (jnp.cos(angles)[:, None, :], jnp.sin(angles)[:, None, :], growth[:, None, :])


def rotate(vectors, cosine, sine_table, factor):
    half_width = vectors.shape[-1] // 2
    first_half = vectors[..., :half_width]
    second_half = vectors[..., half_width:]
    return jnp.concatenate(
        [
            (first_half * cosine - second_half * sine_table) * factor,
            (second_half * cosine + first_half * sine_table) * factor,
        ],
        axis=-1,
    )


def rotate_back(grads_rot, cosine, sine_table, factor):
    half_width = grads_rot.shape[-1] // 2
    first_grad = grads_rot[..., :half_width] * factor
    second_grad = grads_rot[..., half_width:] * factor
    return jnp.concatenate(
        [
            first_grad * cosine + second_grad * sine_table,
            second_grad * cosine - first_grad * sine_table,
        ],
        axis=-1,
    )


def norm_full(values, gain_vec, offset_vec):
    center = values - jnp.mean(values, axis=-1, keepdims=True)
    inv_std = lax.rsqrt(jnp.mean(center * center, axis=-1, keepdims=True) + epsilon)
    unit_part = center * inv_std
    return (unit_part * gain_vec + offset_vec, unit_part, inv_std)


def norm_full_back(grad_out, unit_part, inv_std, gain_vec):
    scaled = grad_out * gain_vec
    return inv_std * (
        scaled
        - jnp.mean(scaled, axis=-1, keepdims=True)
        - unit_part * jnp.mean(scaled * unit_part, axis=-1, keepdims=True)
    )


def per_device(
    tokens,
    segment_kind,
    document,
    type_table,
    attend_gain,
    attend_bias,
    input_weight,
    input_bias,
    inner_gain,
    inner_bias,
    output_weight,
    output_bias,
    feed_gain,
    feed_bias,
    up_weight,
    up_bias,
    hidden_gain,
    hidden_bias,
    down_weight,
    down_bias,
    cotangent,
):
    local_rows = tokens.shape[0]
    seq_count = lax.axis_size("seq")
    total_rows = local_rows * seq_count
    local_width = input_weight.shape[2]
    local_heads = local_width // HEAD_DIM
    score_scale = HEAD_DIM ** (-0.5)
    first_row = lax.axis_index("seq") * local_rows
    query_pos = first_row + jnp.arange(local_rows, dtype=jnp.int32)
    query_doc = lax.dynamic_slice_in_dim(document, first_row, local_rows)
    key_pos = jnp.arange(total_rows, dtype=jnp.int32)
    allowed = (query_doc[:, None] == document[None, :]) & (key_pos[None, :] <= query_pos[:, None])
    one_hot = (segment_kind[:, None] == jnp.arange(3, dtype=jnp.int32)[None, :]).astype(
        jnp.bfloat16
    )
    stream = tokens.astype(jnp.float32) + jnp.dot(
        one_hot, type_table, preferred_element_type=jnp.float32
    )
    attend_gain_f = attend_gain.astype(jnp.float32)
    attend_norm, attend_unit, attend_inv = norm_full(
        stream, attend_gain_f, attend_bias.astype(jnp.float32)
    )
    normed_low = attend_norm.astype(jnp.bfloat16)
    projected = (
        jnp.einsum("td,sdf->tsf", normed_low, input_weight, preferred_element_type=jnp.float32)
        + input_bias.astype(jnp.float32)[None]
    )
    cosine, sine_table, growth = xpos_tables(query_pos, HEAD_DIM, total_rows)
    head_shape = (local_rows, local_heads, HEAD_DIM)
    queries = rotate(projected[:, 0].reshape(head_shape), cosine, sine_table, growth).astype(
        jnp.bfloat16
    )
    keys_local = (
        rotate(projected[:, 1].reshape(head_shape), cosine, sine_table, 1.0 / growth)
        .astype(jnp.bfloat16)
        .reshape(local_rows, local_width)
    )
    values_local = projected[:, 2].astype(jnp.bfloat16)
    keys_all, values_all = (
        lax.all_gather(keys_local, "seq", axis=0, tiled=True),
        lax.all_gather(values_local, "seq", axis=0, tiled=True),
    )
    key_heads = keys_all.reshape(total_rows, local_heads, HEAD_DIM).transpose(1, 0, 2)
    value_heads = values_all.reshape(total_rows, local_heads, HEAD_DIM).transpose(1, 0, 2)

    def attend_head(pieces):
        query_one, key_one, value_one = pieces
        scores = (
            jnp.einsum("qd,kd->qk", query_one, key_one, preferred_element_type=jnp.float32)
            * score_scale
        )
        scores = jnp.where(allowed, scores, masked_score)
        top_score = jnp.max(scores, axis=-1, keepdims=True)
        exp_terms = jnp.exp(scores - top_score)
        row_total = jnp.sum(exp_terms, axis=-1, keepdims=True)
        soft_weights = (exp_terms / row_total).astype(jnp.bfloat16)
        head_out = jnp.einsum(
            "qk,kd->qd", soft_weights, value_one, preferred_element_type=jnp.float32
        )
        return (head_out, (top_score + jnp.log(row_total))[:, 0])

    head_outs, log_totals = lax.map(
        attend_head, (queries.transpose(1, 0, 2), key_heads, value_heads)
    )
    mixed_three = head_outs.transpose(1, 0, 2)
    mixed = mixed_three.reshape(local_rows, local_width)
    inner_sum, inner_square = lax.psum(
        (jnp.sum(mixed, axis=-1), jnp.sum(mixed * mixed, axis=-1)), "ffn"
    )
    inner_mean = (inner_sum / D)[:, None]
    inner_inv = lax.rsqrt(inner_square[:, None] / D - inner_mean * inner_mean + epsilon)
    inner_unit = (mixed - inner_mean) * inner_inv
    inner_gain_f = inner_gain.astype(jnp.float32)
    inner_low = (inner_unit * inner_gain_f + inner_bias.astype(jnp.float32)).astype(jnp.bfloat16)
    branch_part = jnp.dot(inner_low, output_weight, preferred_element_type=jnp.float32)
    branch_sum = lax.psum(branch_part, "ffn")
    middle = stream + branch_sum + output_bias.astype(jnp.float32)
    feed_gain_f = feed_gain.astype(jnp.float32)
    feed_norm, feed_unit, feed_inv = norm_full(middle, feed_gain_f, feed_bias.astype(jnp.float32))
    feed_low = feed_norm.astype(jnp.bfloat16)
    pre_act = jnp.dot(feed_low, up_weight, preferred_element_type=jnp.float32) + up_bias.astype(
        jnp.float32
    )
    activated, gelu_back = jax.vjp(partial(jax.nn.gelu, approximate=False), pre_act)
    hidden_sum, hidden_square = lax.psum(
        (jnp.sum(activated, axis=-1), jnp.sum(activated * activated, axis=-1)), "ffn"
    )
    hidden_mean = (hidden_sum / FF)[:, None]
    hidden_inv = lax.rsqrt(hidden_square[:, None] / FF - hidden_mean * hidden_mean + epsilon)
    hidden_unit = (activated - hidden_mean) * hidden_inv
    hidden_gain_f = hidden_gain.astype(jnp.float32)
    hidden_low = (hidden_unit * hidden_gain_f + hidden_bias.astype(jnp.float32)).astype(
        jnp.bfloat16
    )
    feed_part = jnp.dot(hidden_low, down_weight, preferred_element_type=jnp.float32)
    feed_sum = lax.psum(feed_part, "ffn")
    result = (middle + feed_sum + down_bias.astype(jnp.float32)).astype(jnp.bfloat16)
    grad_result = cotangent.astype(jnp.float32)
    grad_down_weight = jnp.einsum(
        "tf,td->fd", hidden_low, cotangent, preferred_element_type=jnp.float32
    )
    grad_down_bias = jnp.sum(grad_result, axis=0)
    grad_hidden_out = jnp.einsum(
        "td,fd->tf", cotangent, down_weight, preferred_element_type=jnp.float32
    )
    grad_hidden_gain = jnp.sum(grad_hidden_out * hidden_unit, axis=0)
    grad_hidden_bias = jnp.sum(grad_hidden_out, axis=0)
    hidden_scaled = grad_hidden_out * hidden_gain_f
    hidden_first, hidden_cross = lax.psum(
        (jnp.sum(hidden_scaled, axis=-1), jnp.sum(hidden_scaled * hidden_unit, axis=-1)), "ffn"
    )
    grad_activated = hidden_inv * (
        hidden_scaled - hidden_first[:, None] / FF - hidden_unit * hidden_cross[:, None] / FF
    )
    grad_pre_low = gelu_back(grad_activated)[0].astype(jnp.bfloat16)
    grad_up_weight = jnp.einsum(
        "td,tf->df", feed_low, grad_pre_low, preferred_element_type=jnp.float32
    )
    grad_up_bias = jnp.sum(grad_pre_low.astype(jnp.float32), axis=0)
    feed_back_part = jnp.einsum(
        "tf,df->td", grad_pre_low, up_weight, preferred_element_type=jnp.float32
    )
    grad_feed_out = lax.psum(feed_back_part, "ffn")
    grad_feed_gain = jnp.sum(grad_feed_out * feed_unit, axis=0)
    grad_feed_bias = jnp.sum(grad_feed_out, axis=0)
    grad_middle = grad_result + norm_full_back(grad_feed_out, feed_unit, feed_inv, feed_gain_f)
    feed_grads = (
        grad_up_weight,
        grad_up_bias,
        grad_hidden_gain,
        grad_hidden_bias,
        grad_down_weight,
        grad_down_bias,
        grad_feed_gain,
        grad_feed_bias,
    )
    grad_branch_low = grad_middle.astype(jnp.bfloat16)
    grad_output_weight = jnp.einsum(
        "tf,td->fd", inner_low, grad_branch_low, preferred_element_type=jnp.float32
    )
    grad_output_bias = jnp.sum(grad_branch_low.astype(jnp.float32), axis=0)
    grad_inner_out = jnp.einsum(
        "td,fd->tf", grad_branch_low, output_weight, preferred_element_type=jnp.float32
    )
    grad_inner_gain = jnp.sum(grad_inner_out * inner_unit, axis=0)
    grad_inner_bias = jnp.sum(grad_inner_out, axis=0)
    inner_scaled = grad_inner_out * inner_gain_f
    inner_first, inner_cross = lax.psum(
        (jnp.sum(inner_scaled, axis=-1), jnp.sum(inner_scaled * inner_unit, axis=-1)), "ffn"
    )
    grad_mixed = inner_inv * (
        inner_scaled - inner_first[:, None] / D - inner_unit * inner_cross[:, None] / D
    )
    grad_mixed_low = grad_mixed.astype(jnp.bfloat16)
    grad_heads = grad_mixed_low.reshape(head_shape)
    row_delta = jnp.sum(
        grad_mixed_low.astype(jnp.float32).reshape(head_shape) * mixed_three, axis=-1
    ).T

    def key_block_grads(key_block, value_block, key_start):
        block_rows = key_block.shape[0]
        key_three = key_block.reshape(block_rows, local_heads, HEAD_DIM)
        value_three = value_block.reshape(block_rows, local_heads, HEAD_DIM)
        block_pos = key_start + jnp.arange(block_rows, dtype=jnp.int32)
        block_doc = lax.dynamic_slice_in_dim(document, key_start, block_rows)
        block_mask = (query_doc[:, None] == block_doc[None, :]) & (
            block_pos[None, :] <= query_pos[:, None]
        )
        scores = (
            jnp.einsum("qhd,khd->hqk", queries, key_three, preferred_element_type=jnp.float32)
            * score_scale
        )
        full_weights = jnp.where(block_mask[None], jnp.exp(scores - log_totals[:, :, None]), 0.0)
        grad_weights = jnp.einsum(
            "qhd,khd->hqk", grad_heads, value_three, preferred_element_type=jnp.float32
        )
        grad_scores = (full_weights * (grad_weights - row_delta[:, :, None])).astype(jnp.bfloat16)
        query_part = jnp.einsum(
            "hqk,khd->qhd", grad_scores, key_three, preferred_element_type=jnp.float32
        )
        key_part = (
            jnp.einsum("hqk,qhd->khd", grad_scores, queries, preferred_element_type=jnp.float32)
            * score_scale
        )
        value_part = jnp.einsum(
            "hqk,qhd->khd",
            full_weights.astype(jnp.bfloat16),
            grad_heads,
            preferred_element_type=jnp.float32,
        )
        return (
            query_part,
            key_part.reshape(block_rows, local_width),
            value_part.reshape(block_rows, local_width),
        )

    block_group = math.gcd(seq_count, 4)
    group_rows = local_rows * block_group
    zero_query = jnp.zeros(head_shape, jnp.float32)
    zero_buffer = jnp.zeros((total_rows, local_width), jnp.float32)
    key_piece = lax.all_gather(keys_local, "seq", axis=0, tiled=True)
    value_piece = lax.all_gather(values_local, "seq", axis=0, tiled=True)
    piece_rows = key_piece.shape[0]
    sub_rows = math.gcd(piece_rows, group_rows)

    def sub_step(inner_running, sub_index):
        query_acc, key_buffer, value_buffer = inner_running
        offset = sub_index * sub_rows
        key_block = lax.dynamic_slice_in_dim(key_piece, offset, sub_rows)
        value_block = lax.dynamic_slice_in_dim(value_piece, offset, sub_rows)
        query_part, key_part, value_part = key_block_grads(key_block, value_block, offset)
        key_buffer = lax.dynamic_update_slice_in_dim(key_buffer, key_part, offset, 0)
        value_buffer = lax.dynamic_update_slice_in_dim(value_buffer, value_part, offset, 0)
        return ((query_acc + query_part, key_buffer, value_buffer), None)

    updated, unused_steps = lax.scan(
        sub_step,
        (zero_query, zero_buffer, zero_buffer),
        jnp.arange(piece_rows // sub_rows, dtype=jnp.int32),
    )
    query_sum, grad_keys_all, grad_values_all = updated
    grad_keys_own, grad_values_own = (
        lax.psum_scatter(grad_keys_all, "seq", scatter_dimension=0, tiled=True),
        lax.psum_scatter(grad_values_all, "seq", scatter_dimension=0, tiled=True),
    )
    grad_query_lin = rotate_back(query_sum * score_scale, cosine, sine_table, growth)
    grad_key_lin = rotate_back(grad_keys_own.reshape(head_shape), cosine, sine_table, 1.0 / growth)
    grad_projected = jnp.stack(
        [
            grad_query_lin.reshape(local_rows, local_width),
            grad_key_lin.reshape(local_rows, local_width),
            grad_values_own,
        ],
        axis=1,
    ).astype(jnp.bfloat16)
    grad_input_weight = jnp.einsum(
        "td,tsf->sdf", normed_low, grad_projected, preferred_element_type=jnp.float32
    )
    grad_input_bias = jnp.sum(grad_projected.astype(jnp.float32), axis=0)
    normed_back_part = jnp.einsum(
        "tsf,sdf->td", grad_projected, input_weight, preferred_element_type=jnp.float32
    )
    grad_normed = lax.psum(normed_back_part, "ffn")
    grad_attend_gain = jnp.sum(grad_normed * attend_unit, axis=0)
    grad_attend_bias = jnp.sum(grad_normed, axis=0)
    grad_tokens = grad_middle + norm_full_back(grad_normed, attend_unit, attend_inv, attend_gain_f)
    grad_type_table = jnp.einsum(
        "tc,td->cd", one_hot.astype(jnp.float32), grad_tokens, precision=highest
    )
    attention_grads = (
        grad_type_table,
        grad_attend_gain,
        grad_attend_bias,
        grad_input_weight,
        grad_input_bias,
        grad_inner_gain,
        grad_inner_bias,
        grad_output_weight,
        grad_output_bias,
    )
    summed = lax.psum(feed_grads + attention_grads, "seq")
    feed_grads = summed[:8]
    attention_grads = summed[8:]
    return (
        result,
        grad_tokens,
        attention_grads[0],
        attention_grads[1],
        attention_grads[2],
        attention_grads[3],
        attention_grads[4],
        attention_grads[5],
        attention_grads[6],
        attention_grads[7],
        attention_grads[8],
        feed_grads[6],
        feed_grads[7],
        feed_grads[0],
        feed_grads[1],
        feed_grads[2],
        feed_grads[3],
        feed_grads[4],
        feed_grads[5],
    )


def solution(mesh):
    in_specs = (
        P("seq", None),
        P("seq"),
        P(),
        P(),
        P(),
        P(),
        P(None, None, "ffn"),
        P(None, "ffn"),
        P("ffn"),
        P("ffn"),
        P("ffn", None),
        P(),
        P(),
        P(),
        P(None, "ffn"),
        P("ffn"),
        P("ffn"),
        P("ffn"),
        P("ffn", None),
        P(),
        P("seq", None),
    )
    out_specs = (
        P("seq", None),
        P("seq", None),
        P(),
        P(),
        P(),
        P(None, None, "ffn"),
        P(None, "ffn"),
        P("ffn"),
        P("ffn"),
        P("ffn", None),
        P(),
        P(),
        P(),
        P(None, "ffn"),
        P("ffn"),
        P("ffn"),
        P("ffn"),
        P("ffn", None),
        P(),
    )
    return jax.shard_map(
        per_device, mesh=mesh, in_specs=in_specs, out_specs=out_specs, check_vma=False
    )
```

profile of v0, /device:TPU:0, one launch (start us, length us, event | category | flops | bytes accessed | tf_op | source)
XLA Modules:
  0.0 1401.0 jit_solution(6520882346358691108)
XLA Ops:
  9.5 1.5 fusion.60
  12.0 2.3 convolution_add_fusion.2
  17.7 138.4 %all-gather.4.cloned.1.call-done = bf16[8192,256]{0,1:T(8,128)(2,1)} async-done(((bf16[256,256]{0,1:T(8,128)(2,1)}), bf16[8192,256]{0,1:T(8,128)(2,1)}) %all-gather.4.cloned.1.call-update) | async-done | bytes 4194320 | tf_op jit(solution)/shard_map/all_gather | solution.py:134
  156.1 8.4 copy.56
  164.5 132.3 %all-gather.6.cloned.1.call-done = bf16[8192,1,256]{0,2,1:T(8,128)(2,1)} async-done(((bf16[256,1,256]{0,2,1:T(8,128)(2,1)}), bf16[8192,1,256]{0,2,1:T(8,128)(2,1)}) %all-gather.6.cloned.1.call-update) | async-done | bytes 4194320 | tf_op jit(solution)/shard_map/all_gather | solution.py:135
  296.8 8.4 copy.57
  305.2 42.6 %while.28 = (s32[]{:T(128)}, f32[4,256,64]{1,2,0:T(8,128)S(1)}, f32[4,256]{1,0:T(4,128)}, bf16[4,256,64]{1,2,0:T(8,128)(2,1)S(1)}, bf16[4,8192,64]{2,1,0:T(8,128...) while((s32[]{:T(128)}, f32[4,256,64]{1,2,0:T(8,128)S(1)}, ...), condition=%wide.region_5.6_spmd.clone, body=%wide.region_2.5_spmd.clone.sunk | while | flops 559939328 | bytes 29505656 | solution.py:156
  305.3 4.5 fusion.108
  311.1 3.5 fusion.110
  315.9 4.5 fusion.108
  321.8 3.5 fusion.110
  326.6 4.5 fusion.108
  332.4 3.5 fusion.110
  337.2 4.5 fusion.108
  343.0 3.5 fusion.110
  347.9 7.2 all-reduce.5
  356.8 46.2 %all-reduce.12.cloned.1.call-done = f32[256,1024]{1,0:T(8,128)} async-done(((f32[256,1024]{1,0:T(8,128)}), f32[256,1024]{1,0:T(8,128)}) %all-reduce.12.cloned.1.call-update) | async-done | bytes 1048592 | tf_op jit(solution)/shard_map/psum | solution.py:170
  403.0 1.7 fusion.57
  405.0 4.3 fusion.55
  409.4 8.8 all-reduce.4
  418.1 4.5 multiply_reduce_fusion
  422.7 7.1 all-reduce.3
  429.8 3.6 convert_reduce_fusion.1
  434.2 1.7 fusion.63
  436.0 45.5 %all-reduce.14.cloned.1.call-done = f32[256,1024]{1,0:T(8,128)} async-done(((f32[256,1024]{1,0:T(8,128)}), f32[256,1024]{1,0:T(8,128)}) %all-reduce.14.cloned.1.call-update) | async-done | bytes 1048592 | tf_op jit(solution)/shard_map/psum | solution.py:217
  481.5 2.3 multiply_reduce_fusion.1
  483.8 2.5 convert_reduce_fusion.2
  488.4 8.6 all-reduce.2
  498.8 4.2 broadcast_in_dim.28
  503.0 3.8 broadcast_in_dim.28.clone
  506.8 91.6 %while.29 = (s32[]{:T(128)}, f32[256,4,64]{0,2,1:T(8,128)S(1)}, f32[8192,256]{0,1:T(8,128)}, f32[8192,256]{1,0:T(8,128)}, s32[8]{0:T(128)}, /*index=5*/bf16[8192...) while((s32[]{:T(128)}, f32[256,4,64]{0,2,1:T(8,128)S(1)}, ...), condition=%wide.region_31.32_spmd.clone, body=%wide.region_30.31_spmd.clone.sunk | while | flops 682755328 | bytes 69553672 | solution.py:310
  599.7 3.3 fusion.54
  603.8 174.4 %reduce-scatter.3.cloned.1.call-done = f32[256,256]{0,1:T(8,128)} async-done(((f32[8192,256]{0,1:T(8,128)}), f32[256,256]{0,1:T(8,128)}) %reduce-scatter.3.cloned.1.call-update) | async-done | bytes 262160 | tf_op jit(solution)/shard_map/reduce_scatter | solution.py:317
  778.2 1.8 add_convert_fusion.7
  781.1 175.1 %reduce-scatter.5.cloned.1.call-done = f32[256,256]{1,0:T(8,128)} async-done(((f32[8192,256]{1,0:T(8,128)}), f32[256,256]{1,0:T(8,128)}) %reduce-scatter.5.cloned.1.call-update) | async-done | bytes 262160 | tf_op jit(solution)/shard_map/reduce_scatter | solution.py:318
  957.2 1.6 convolution_bitcast_fusion.2
  959.1 3.6 fusion.52
  962.8 4.5 fusion.53
  968.7 2.4 convolution_bitcast_fusion.1
  972.5 41.3 %all-reduce.18.cloned.1.call-done = (f32[256,1024]{1,0:T(8,128)}, f32[256,1024]{1,0:T(8,128)}) async-done(((f32[256,1024]{1,0:T(8,128)}, f32[256,1024]{1,0:T(8,128)}), (f32[256,1024]{1,0:T(8,128)}, f32[256,1024]{1,0:T(8,128)})) %all-reduce.18.cloned.1.call-update) | async-done | bytes 2097168 | tf_op jit(solution)/shard_map/psum | solution.py:190
  1013.8 1.7 multiply_reduce_fusion.2
  1015.5 1.6 multiply_add_fusion
  1019.3 157.2 %all-reduce = (f32[3,1024]{1,0:T(4,128)}, f32[1024]{0:T(1024)}, f32[1024]{0:T(1024)}, f32[3,256]{1,0:T(4,128)}, f32[256]{0:T(256)}, /*index=5*/f32[256]{0:T(256)...) all-reduce(f32[3,1024]{1,0:T(4,128)S(1)} %fusion.40, ...), channel_id=1, replica_groups=mesh['seq'=32,'ffn'=4] {'seq'}, use_global_device_ids=true, to_apply=%region_37.38 | all-reduce | flops 13568 | bytes 108544 | tf_op jit(solution)/shard_map/psum | solution.py:355
  1176.5 2.2 add_convert_fusion.1
  1178.7 203.9 %all-reduce.16.cloned.1.call-done = (f32[3,1024,256]{1,2,0:T(8,128)}, f32[256,1024]{1,0:T(8,128)}, f32[1024,1024]{1,0:T(8,128)}, f32[1024,1024]{1,0:T(8,128)}) async-done(((f32[3,1024,256]{1,2,0:T(8,128)}, f32[256,1024]{1,0:T(8,128)}, f32[1024,1024]{1,0:T(8,128)}, f32[1024,1024]{1,0:T(8,128)}), (f32[3,1024,256]{1,2,0:T(8,128)}, f32[256,1024]{1,0:T(8,128)}, f32[1024,1024]{1,0:T(8,128)}, ...) | async-done | bytes 12582928 | tf_op jit(solution)/shard_map/psum | solution.py:355
  1382.6 3.6 copy.63
  1387.2 4.9 copy.137
  1392.2 2.0 copy.138
  (464 shorter events, 119.1 us)
Async XLA Ops:
  7.2 397.8 %copy-start = (bf16[1024,1024]{1,0:T(8,128)(2,1)S(1)}, bf16[1024,1024]{1,0:T(8,128)(2,1)}, u32[]{:S(2)}) copy-start(bf16[1024,1024]{1,0:T(8,128)(2,1)} %param.39) | copy-start | bytes 6291460
  7.2 148.9 %all-gather.4.cloned.1.call-start = ((), (), s32[]{:S(2)}) async-start(), calls=%async_computation.2 | async-start | bytes 4325376 | tf_op jit(solution)/shard_map/all_gather | solution.py:134
  8.8 6.0 copy-start.45
  9.5 5.4 copy-start.35
  11.0 5.9 copy-start.68
  11.0 5.9 copy-start.69
  11.0 5.0 copy-start.37
  16.0 280.7 %all-gather.6.cloned.1.call-start = ((), (), s32[]{:S(2)}) async-start(), calls=%async_computation.7 | async-start | bytes 4325376 | tf_op jit(solution)/shard_map/all_gather | solution.py:135
  16.8 386.2 %all-reduce.12.cloned.1.call-start = ((), (), s32[]{:S(2)}) async-start(), calls=%async_computation.3 | async-start | bytes 2097152 | tf_op jit(solution)/shard_map/psum | solution.py:170
  16.9 338.2 %copy-start.53 = (f32[256]{0:T(256)}, f32[256]{0:T(256)S(1)}, u32[]{:S(2)}) copy-start(f32[256]{0:T(256)S(1)} %convert_element_type.123) | copy-start | bytes 3076
  305.2 50.1 %copy-start.19 = (bf16[256,1024]{1,0:T(8,128)(2,1)S(1)}, bf16[256,1024]{1,0:T(8,128)(2,1)}, u32[]{:S(2)}) copy-start(bf16[256,1024]{1,0:T(8,128)(2,1)} %param.35) | copy-start | bytes 1572868
  305.2 51.5 %copy-start.60 = (bf16[1024]{0:T(1024)(128)(2,1)S(1)}, bf16[1024]{0:T(1024)(128)(2,1)}, u32[]{:S(2)}) copy-start(bf16[1024]{0:T(1024)(128)(2,1)} %param.36) | copy-start | bytes 6148
  305.2 51.5 %copy-start.61 = (bf16[1024]{0:T(1024)(128)(2,1)S(1)}, bf16[1024]{0:T(1024)(128)(2,1)}, u32[]{:S(2)}) copy-start(bf16[1024]{0:T(1024)(128)(2,1)} %param.40) | copy-start | bytes 6148
  305.2 51.5 %copy-start.62 = (bf16[1024]{0:T(1024)(128)(2,1)S(1)}, bf16[1024]{0:T(1024)(128)(2,1)}, u32[]{:S(2)}) copy-start(bf16[1024]{0:T(1024)(128)(2,1)} %param.38) | copy-start | bytes 6148
  305.2 51.5 %copy-start.63 = (bf16[1024]{0:T(1024)(128)(2,1)S(1)}, bf16[1024]{0:T(1024)(128)(2,1)}, u32[]{:S(2)}) copy-start(bf16[1024]{0:T(1024)(128)(2,1)} %param.37) | copy-start | bytes 6148
  305.2 51.5 %copy-start.64 = (bf16[1024]{0:T(1024)(128)(2,1)S(1)}, bf16[1024]{0:T(1024)(128)(2,1)}, u32[]{:S(2)}) copy-start(bf16[1024]{0:T(1024)(128)(2,1)} %param.41) | copy-start | bytes 6148
  347.8 8.9 copy-start.10
  356.6 124.8 %all-reduce.14.cloned.1.call-start = ((), (), s32[]{:S(2)}) async-start(), calls=%async_computation.4 | async-start | bytes 2097152 | tf_op jit(solution)/shard_map/psum | solution.py:217
  356.7 52.6 %copy-start.47 = (f32[1024]{0:T(1024)}, f32[1024]{0:T(1024)S(1)}, u32[]{:S(2)}) copy-start(f32[1024]{0:T(1024)S(1)} %convert_element_type.128) | copy-start | bytes 12292
  404.7 79.1 %copy-start.4 = (f32[256,1024]{1,0:T(8,128)}, f32[256,1024]{1,0:T(8,128)S(1)}, u32[]{:S(2)}) copy-start(f32[256,1024]{1,0:T(8,128)S(1)} %get-tuple-element.363) | copy-start | bytes 3145732
  418.1 15.2 %copy-start.55 = (f32[256]{0:T(256)}, f32[256]{0:T(256)S(1)}, u32[]{:S(2)}) copy-start(f32[256]{0:T(256)S(1)} %get-tuple-element.387) | copy-start | bytes 3076
  418.1 15.2 %copy-start.57 = (f32[256]{0:T(256)}, f32[256]{0:T(256)S(1)}, u32[]{:S(2)}) copy-start(f32[256]{0:T(256)S(1)} %get-tuple-element.388) | copy-start | bytes 3076
  435.9 51.4 %copy-start.11 = (f32[4,256,64]{1,2,0:T(8,128)S(1)}, f32[4,256,64]{1,2,0:T(8,128)}, u32[]{:S(2)}) copy-start(f32[4,256,64]{1,2,0:T(8,128)} %copy-done.10) | copy-start | bytes 786436
  435.9 51.4 %copy-start.20 = (bf16[256,1024]{1,0:T(8,128)(2,1)S(1)}, bf16[256,1024]{1,0:T(8,128)(2,1)}, u32[]{:S(2)}) copy-start(bf16[256,1024]{1,0:T(8,128)(2,1)} %param.35) | copy-start | bytes 1572868
  435.9 51.4 %copy-start.40 = (f32[256]{0:T(256)S(1)}, f32[256]{0:T(256)}, u32[]{:S(2)}) copy-start(f32[256]{0:T(256)} %copy-done.39) | copy-start | bytes 3076
  435.9 51.4 %copy-start.42 = (f32[256]{0:T(256)S(1)}, f32[256]{0:T(256)}, u32[]{:S(2)}) copy-start(f32[256]{0:T(256)} %copy-done.41) | copy-start | bytes 3076
  435.9 51.4 %copy-start.54 = (f32[256]{0:T(256)S(1)}, f32[256]{0:T(256)}, u32[]{:S(2)}) copy-start(f32[256]{0:T(256)} %copy-done.53) | copy-start | bytes 3076
  435.9 342.2 %reduce-scatter.3.cloned.1.call-start = ((), (), s32[]{:S(2)}) async-start(), calls=%async_computation.5 | async-start | bytes 8650752 | tf_op jit(solution)/shard_map/reduce_scatter | solution.py:317
  598.4 357.9 %reduce-scatter.5.cloned.1.call-start = ((), (), s32[]{:S(2)}) async-start(), calls=%async_computation.6 | async-start | bytes 8650752 | tf_op jit(solution)/shard_map/reduce_scatter | solution.py:318
  599.0 179.2 %copy-start.26 = (f32[256,32]{0,1:T(8,128)S(1)}, f32[256,32]{0,1:T(8,128)}, u32[]{:S(2)}) copy-start(f32[256,32]{0,1:T(8,128)} %copy-done.25) | copy-start | bytes 98308
  599.0 179.2 %copy-start.28 = (f32[256,32]{0,1:T(8,128)S(1)}, f32[256,32]{0,1:T(8,128)}, u32[]{:S(2)}) copy-start(f32[256,32]{0,1:T(8,128)} %copy-done.27) | copy-start | bytes 98308
  599.0 179.2 %copy-start.30 = (f32[256,32]{0,1:T(8,128)S(1)}, f32[256,32]{0,1:T(8,128)}, u32[]{:S(2)}) copy-start(f32[256,32]{0,1:T(8,128)} %copy-done.29) | copy-start | bytes 98308
  599.0 179.2 %copy-start.32 = (f32[256,32]{0,1:T(8,128)S(1)}, f32[256,32]{0,1:T(8,128)}, u32[]{:S(2)}) copy-start(f32[256,32]{0,1:T(8,128)} %copy-done.31) | copy-start | bytes 98308
  599.0 358.2 %copy-start.21 = (bf16[3,1024,256]{2,1,0:T(8,128)(2,1)S(1)}, bf16[3,1024,256]{2,1,0:T(8,128)(2,1)}, u32[]{:S(2)}) copy-start(bf16[3,1024,256]{2,1,0:T(8,128)(2,1)} %param.31) | copy-start | bytes 4718596
  599.0 414.8 %all-reduce.18.cloned.1.call-start = ((), (), s32[]{:S(2)}) async-start(), calls=%async_computation.9 | async-start | bytes 4194304 | tf_op jit(solution)/shard_map/psum | solution.py:190
  603.1 356.0 %copy-start.5 = (f32[256,1024]{1,0:T(8,128)S(1)}, f32[256,1024]{1,0:T(8,128)}, u32[]{:S(2)}) copy-start(f32[256,1024]{1,0:T(8,128)} %copy-done.4) | copy-start | bytes 3145732
  603.1 356.1 %copy-start.15 = (bf16[256,1024]{1,0:T(8,128)(2,1)S(1)}, bf16[256,1024]{1,0:T(8,128)(2,1)}, u32[]{:S(2)}) copy-start(bf16[256,1024]{1,0:T(8,128)(2,1)} %copy-done.14) | copy-start | bytes 1572868
  603.1 356.1 %copy-start.48 = (f32[1024]{0:T(1024)S(1)}, f32[1024]{0:T(1024)}, u32[]{:S(2)}) copy-start(f32[1024]{0:T(1024)} %copy-done.47) | copy-start | bytes 12292
  958.8 423.8 %all-reduce.16.cloned.1.call-start = ((), (), s32[]{:S(2)}) async-start(), calls=%async_computation.8 | async-start | bytes 25165824 | tf_op jit(solution)/shard_map/psum | solution.py:355
  962.7 5.9 copy-start.7
  962.7 5.9 copy-start.36
  962.7 5.9 copy-start.38
  962.7 5.9 copy-start.46
  962.7 5.9 copy-start.52
  971.1 48.1 %copy-start.43 = (f32[1024]{0:T(1024)S(1)}, f32[1024]{0:T(1024)}, u32[]{:S(2)}) copy-start(f32[1024]{0:T(1024)} %get-tuple-element.265) | copy-start | bytes 12292
  972.5 46.8 %copy-start.44 = (f32[3,256]{1,0:T(4,128)S(1)}, f32[3,256]{1,0:T(4,128)}, u32[]{:S(2)}) copy-start(f32[3,256]{1,0:T(4,128)} %convert_reduce_fusion.3) | copy-start | bytes 9220
  1387.2 4.9 copy-start.16
  1387.2 7.0 copy-start.1
  (93 other events, 223.6 us)
Sparse Core Ops, SparseCore 0:
  16.2 139.8 all-gather.3
  158.2 138.4 all-gather.5
  356.7 46.2 all-reduce.11
  436.0 45.3 all-reduce.13
  598.5 179.5 reduce-scatter.2
  780.4 175.7 reduce-scatter.4
  959.0 54.7 all-reduce.17
  1018.5 364.0 all-reduce.15
where the time goes:
time: 1400 us
  waiting for transfers between devices  958 us (68%)
  blocking collectives  189 us (14%)
  matrix products  102 us (7%)
  local copies, waits for them, and re-layouts  94.9 us (7%)
  other arithmetic  35 us (2%)
  between operations  14.9 us (1%)
    psum x1, waiting for transfers between devices, per_device(): summed = lax.psum(feed_grads + attention_grads, 'seq')  204 us
    reduce_scatter x1, waiting for transfers between devices, per_device(): lax.psum_scatter(grad_values_all, 'seq', scatter_dimension=0, tiled=True)  175 us
    reduce_scatter x1, waiting for transfers between devices, per_device(): lax.psum_scatter(grad_keys_all, 'seq', scatter_dimension=0, tiled=True)  174 us
    psum x1, blocking collectives, per_device(): summed = lax.psum(feed_grads + attention_grads, 'seq')  157 us
    all_gather x1, waiting for transfers between devices, per_device(): lax.all_gather(keys_local, 'seq', axis=0, tiled=True)  138 us
    all_gather x1, waiting for transfers between devices, per_device(): lax.all_gather(values_local, 'seq', axis=0, tiled=True)  132 us
    psum x1, waiting for transfers between devices, per_device(): branch_sum = lax.psum(branch_part, 'ffn')  46.2 us
    psum x1, waiting for transfers between devices, per_device(): grad_feed_out = lax.psum(feed_back_part, 'ffn')  45.5 us
  transfers between devices with their start and end apart: 8, of which 8 were waited for; matrix products, arithmetic and copies ran while one was open for 3% of the time, Pallas kernels for 0%

commit v1 on v0

v1 whole, which is shorter than its diff:
```python
from functools import partial
import math

import jax
import jax.numpy as jnp
from jax import lax
from jax.experimental import pallas as pl
from jax.experimental.pallas import tpu as pltpu
from jax.sharding import PartitionSpec as P

D = 1024
FF = 4096
HEAD_DIM = 64
ROW = 1024
PACK = ROW // 2
PLANE = 4

epsilon = 1e-05
scale_base = 512.0
masked_score = -1e30
log2_e = 1.4426950408889634
score_factor = HEAD_DIM ** (-0.5) * log2_e
highest = lax.Precision.HIGHEST
f32 = jnp.float32
bf16 = jnp.bfloat16


def seq_index(y, z, x):
    return (y % 4) * 8 + (z % 2) * 4 + x % 4


def seq_pairs(move):
    pairs = []
    for y in range(4):
        for z in range(2):
            for x in range(4):
                pairs.append((seq_index(y, z, x), seq_index(*move(y, z, x))))
    return pairs


def shift_pairs(dy, dz, dx):
    return seq_pairs(lambda y, z, x: (y + dy, z + dz, x + dx))


def group_of(row):
    return min(row, 7 - row)


TO_SAME = seq_pairs(lambda y, z, x: (group_of(2 * y + z), z, x))
TO_OTHER = seq_pairs(lambda y, z, x: (group_of(2 * y + z), 1 - z, x))
FROM_SAME = [(b, a) for a, b in TO_SAME]
FROM_OTHER = [(b, a) for a, b in TO_OTHER]
X_SHIFTS = [shift_pairs(0, 0, d) for d in (1, 2, 3)]
Y_SHIFTS = [shift_pairs(d, 0, 0) for d in (1, 2, 3)]
Z_SWAP = shift_pairs(0, 1, 0)
CORE_SWAP = [(f, f ^ 1) for f in range(4)]
FAR_SWAP = [(f, f ^ 2) for f in range(4)]
Y_GROUPS = [[seq_index(y, z, x) for y in range(4)] for z in range(2) for x in range(4)]
X_GROUPS = [[seq_index(y, z, x) for x in range(4)] for y in range(4) for z in range(2)]
Z_GROUPS = [[seq_index(y, z, x) for z in range(2)] for y in range(4) for x in range(4)]
YX_GROUPS = [[seq_index(y, z, x) for y in range(4) for x in range(4)] for z in range(2)]


def shift_x(pieces):
    return [lax.ppermute(piece, "seq", pairs) for piece, pairs in zip(pieces[1:], X_SHIFTS)]


def shift_y(pieces):
    return [lax.ppermute(piece, "seq", pairs) for piece, pairs in zip(pieces[1:], Y_SHIFTS)]


def core_swap(values):
    return lax.ppermute(values, "ffn", CORE_SWAP)


def far_swap(values):
    return lax.ppermute(values, "ffn", FAR_SWAP)


def gather_x(values):
    return lax.all_gather(values, "seq", axis_index_groups=X_GROUPS, tiled=True)


def share_yx(values):
    values = lax.all_gather(values, "seq", axis_index_groups=YX_GROUPS)
    return values.reshape((4, 4) + values.shape[1:])


def sum_z(values):
    other = lax.ppermute(values, "seq", Z_SWAP)
    return (values.astype(f32) + other.astype(f32)).astype(bf16)


def after(value, *others):
    return lax.optimization_barrier((value,) + others)[0]


X, Y, Z, CORE, PART = range(5)


def run(kernel, name, here, operands, outs, scratch=(), megabytes=8, far=()):
    first = 1 + len(operands)

    def body(*refs):
        refs = list(refs)
        semaphores = refs.pop() if far else None
        kept = refs[len(refs) - len(far) :]
        refs = refs[: len(refs) - len(far)]
        targets = [refs[first + k] for k in far]
        for k, ref in zip(far, kept):
            refs[first + k] = ref
        kernel(*refs)
        copies = [
            pltpu.make_async_copy(ref, target, semaphores.at[k])
            for k, (ref, target) in enumerate(zip(kept, targets))
        ]
        for copy in copies:
            copy.start()
        for copy in copies:
            copy.wait()

    extra = [pltpu.VMEM(*outs[k]) for k in far]
    if far:
        extra.append(pltpu.SemaphoreType.DMA((len(far),)))
    return pl.pallas_call(
        body,
        in_specs=[pl.BlockSpec(memory_space=pltpu.SMEM)]
        + [pl.BlockSpec(memory_space=pltpu.VMEM)] * len(operands),
        out_specs=[
            pl.BlockSpec(memory_space=pltpu.HBM if k in far else pltpu.VMEM) for k in range(len(outs))
        ],
        out_shape=[jax.ShapeDtypeStruct(shape, kind) for shape, kind in outs],
        scratch_shapes=list(scratch) + extra,
        compiler_params=pltpu.CompilerParams(vmem_limit_bytes=megabytes * 2**20),
        cost_estimate=pl.CostEstimate(
            flops=2**20,
            bytes_accessed=sum(v.size * v.dtype.itemsize for v in operands)
            + sum(math.prod(shape) * jnp.dtype(kind).itemsize for shape, kind in outs),
            transcendentals=0,
        ),
        name=name,
    )(here, *operands)


def dot_nn(a, b):
    return lax.dot_general(a, b, (((1,), (0,)), ((), ())), preferred_element_type=f32)


def dot_nt(a, b):
    return lax.dot_general(a, b, (((1,), (1,)), ((), ())), preferred_element_type=f32)


def dot_tn(a, b):
    return lax.dot_general(a, b, (((0,), (0,)), ((), ())), preferred_element_type=f32)


def before(place, d):
    return lax.rem(place + (4 - d), 4)


def store_at(refs, place, index, value):
    for d, ref in enumerate(refs):

        @pl.when(lax.rem(place + d, 4) == index)
        def _(ref=ref):
            ref[...] = value


def store_half(mine, theirs, core, half, value):
    @pl.when(core == half)
    def _():
        mine[...] = value

    @pl.when(core != half)
    def _():
        theirs[...] = value


def row_of(column):
    return jnp.broadcast_to(column, (column.shape[0], 128)).T[0:1]


def split_three(values):
    high = values.astype(bf16).astype(f32)
    middle = (values - high).astype(bf16).astype(f32)
    return high, middle, values - high - middle


def norm_parts(values):
    center = values - jnp.mean(values, axis=-1, keepdims=True)
    inv_std = lax.rsqrt(jnp.mean(center * center, axis=-1, keepdims=True) + epsilon)
    return center * inv_std, inv_std


def norm_back(grad_out, unit, inv_std, gain):
    scaled = grad_out * gain
    return inv_std * (
        scaled
        - jnp.mean(scaled, axis=-1, keepdims=True)
        - unit * jnp.mean(scaled * unit, axis=-1, keepdims=True)
    )


def pair_pack(values, side):
    left = lax.broadcasted_iota(jnp.int32, (128, 128), 1) < 64
    if side == 0:
        return jnp.where(left, values[:128], pltpu.roll(values[128:], 64, 1))
    return jnp.where(left, pltpu.roll(values[:128], 64, 1), values[128:])


def pair_unpack(even, odd):
    left = lax.broadcasted_iota(jnp.int32, (128, 128), 1) < 64
    low = jnp.where(left, even, pltpu.roll(odd, 64, 1))
    high = jnp.where(left, pltpu.roll(even, 64, 1), odd)
    return jnp.concatenate([low, high], axis=0)


def half_swapped(values):
    lane = lax.broadcasted_iota(jnp.int32, values.shape, 1)
    return jnp.where(lane % 64 < 32, pltpu.roll(values, 96, 1), pltpu.roll(values, 32, 1))


def enter_kernel(
    here, tokens, kind, table, gain, offset, weight, shift, cosine, sine, growth, stream_ref, normed_ref, *out
):
    stream = tokens[...].astype(f32)
    for c in range(3):
        stream = stream + jnp.where(kind[...] == c, table[c : c + 1, :].astype(f32), 0.0)
    stream_ref[...] = stream
    unit, _ = norm_parts(stream)
    normed = (unit * gain[...].astype(f32) + offset[...].astype(f32)).astype(bf16)
    normed_ref[...] = normed
    projected = [dot_nn(normed, weight[s]) + shift[s : s + 1, :].astype(f32) for s in range(3)]
    lane = lax.broadcasted_iota(jnp.int32, (256, 128), 1)
    left = lane < 64
    signed = jnp.where(lane % 64 < 32, -sine[...], sine[...])
    for group in range(2):
        lanes = slice(128 * group, 128 * group + 128)
        query, key, value = [p[:, lanes] for p in projected]
        query = (query * cosine[...] + half_swapped(query) * signed) * growth[...]
        key = (key * cosine[...] + half_swapped(key) * signed) / growth[...]
        for side in range(2):
            if side == 0:
                both = jnp.where(left, key, pltpu.roll(value, 64, 1))
            else:
                both = jnp.where(left, pltpu.roll(key, 64, 1), value)
            message = jnp.concatenate([both, pair_pack(query, side)], axis=0).astype(bf16)
            store_at(out, here[X], 2 * group + side, message)


def enter(here, *operands):
    return run(
        enter_kernel,
        "enter",
        here,
        operands,
        [((256, D), f32), ((256, D), bf16)] + [((384, 128), bf16)] * 4,
        megabytes=5, far=(0, 1),
    )


def rows_kernel(here, p0, p1, p2, p3, kv_ref, q_ref):
    for d, ref in enumerate((p0, p1, p2, p3)):
        source = before(here[X], d)
        kv_ref[pl.ds(pl.multiple_of(source * 256, 256), 256), :] = ref[:256, :]
        q_ref[pl.ds(pl.multiple_of(source * 128, 128), 128), :] = ref[256:, :]


def rows(here, *pieces):
    return run(rows_kernel, "rows", here, pieces, [((ROW, 128), bf16), ((PACK, 128), bf16)], megabytes=1)


def lane_rows(row):
    return jnp.concatenate([row[:, 128 * j : 128 * j + 128] for j in range(8)], axis=0)


def unpack_transposed(source, target, offset):
    for b in range(4):
        piece = source[128 * b : 128 * b + 128, :].T
        target[offset : offset + 64, 256 * b : 256 * b + 128] = piece[:64]
        target[offset : offset + 64, 256 * b + 128 : 256 * b + 256] = piece[64:]


def pack_transposed(columns, target):
    for b in range(4):
        piece = jnp.concatenate(
            [columns[:, 256 * b : 256 * b + 128], columns[:, 256 * b + 128 : 256 * b + 256]], axis=0
        )
        target[128 * b : 128 * b + 128, :] = piece.T.astype(target.dtype)


def chunk_bounds(info, tile):
    z = info[0]
    row = info[1 + tile]
    lowest = info[3 + tile]
    first = jnp.int32(0)
    last = jnp.int32(0)
    for c in range(PLANE):
        start = (2 * c + z) * ROW
        first = first + (start + ROW - 1 < lowest).astype(jnp.int32)
        last = last + (2 * c + z <= row).astype(jnp.int32)
    return first, last


def visible(info, tile, c, begin_ref, shape):
    key = (2 * c + info[0]) * ROW + lax.broadcasted_iota(jnp.int32, shape, 0)
    query = info[1 + tile] * ROW + lax.broadcasted_iota(jnp.int32, shape, 1)
    return (key <= query) & (key >= begin_ref[...])


def needs_mask(info, tile, c):
    key_row = 2 * c + info[0]
    return (key_row == info[1 + tile]) | (key_row * ROW < info[5 + tile])


def plane_copies(info, pieces, kv_ref):
    return [
        (piece, kv_ref.at[pl.ds(pl.multiple_of(before(info[7], d) * ROW, ROW), ROW)])
        for d, piece in enumerate(pieces)
    ]


def forward_kernel(
    info,
    qa,
    qb,
    kv0,
    kv1,
    kv2,
    kv3,
    begin_ref,
    outa_ref,
    outb_ref,
    qt_ref,
    q_in,
    kv_ref,
    vt_ref,
    acc_ref,
    top_ref,
    semaphores,
):
    tile = pl.program_id(0)

    @pl.when(tile == 0)
    def _():
        copies = [
            pltpu.make_async_copy(source, target, semaphores.at[k])
            for k, (source, target) in enumerate(
                [(qa, q_in.at[0]), (qb, q_in.at[1])] + plane_copies(info, (kv0, kv1, kv2, kv3), kv_ref)
            )
        ]
        for copy in copies:
            copy.start()
        for copy in copies:
            copy.wait()
        for c in range(PLANE):
            block = kv_ref[c * ROW : c * ROW + ROW, :].T
            index = lax.broadcasted_iota(jnp.int32, block.shape, 0)
            vt_ref[:, c * ROW : c * ROW + ROW] = jnp.where(index < 64, jnp.ones_like(block), block)
        qt_ref[64:, :] = jnp.zeros((64, ROW), bf16)

    unpack_transposed(q_in.at[tile], qt_ref, 0)

    top_ref[...] = jnp.full(top_ref.shape, masked_score, f32)
    acc_ref[...] = jnp.zeros(acc_ref.shape, f32)

    def step(c, masked):
        start = pl.multiple_of(c * ROW, ROW)
        scores = dot_nn(kv_ref[pl.ds(start, ROW), :], qt_ref[...]) * score_factor
        if masked:
            scores = jnp.where(visible(info, tile, c, begin_ref, scores.shape), scores, 2 * masked_score)
        old = top_ref[...]
        top = jnp.maximum(old, jnp.max(scores, axis=0, keepdims=True))
        weights = jnp.exp2(scores - top)
        top_ref[...] = top
        acc_ref[...] = acc_ref[...] * jnp.exp2(old - top) + dot_nn(
            vt_ref[:, pl.ds(start, ROW)], weights.astype(bf16)
        )

    def body(c, carry):
        masked = needs_mask(info, tile, c)

        @pl.when(masked)
        def _():
            step(c, True)

        @pl.when(jnp.logical_not(masked))
        def _():
            step(c, False)

        return carry

    first, last = chunk_bounds(info, tile)
    lax.fori_loop(first, last, body, 0)
    total = acc_ref[0:1, :]
    some = total > 0
    safe = jnp.where(some, total, 1.0)
    log_total = jnp.where(some, top_ref[...] + jnp.log2(safe), masked_score)
    for index, out_ref in enumerate((outa_ref, outb_ref)):

        @pl.when(tile == index)
        def _(out_ref=out_ref):
            pack_transposed(acc_ref[64:, :] / safe, out_ref)
            parts = [lane_rows(part) for part in split_three(log_total)]
            out_ref[PACK:, :] = jnp.concatenate(parts + [jnp.zeros((8, 128), f32)], axis=0).astype(bf16)


def attend_forward(info, queries_a, queries_b, keys_values, begin):
    hbm = pl.BlockSpec(memory_space=pltpu.HBM)
    return pl.pallas_call(
        forward_kernel,
        grid_spec=pltpu.PrefetchScalarGridSpec(
            num_scalar_prefetch=1,
            grid=(2,),
            in_specs=[hbm] * 6 + [pl.BlockSpec((1, ROW), lambda i, s: (0, i))],
            out_specs=[pl.BlockSpec((PACK + 32, 128), lambda i, s: (0, 0))] * 2,
            scratch_shapes=[
                pltpu.VMEM((128, ROW), bf16),
                pltpu.VMEM((2, PACK, 128), bf16),
                pltpu.VMEM((PLANE * ROW, 128), bf16),
                pltpu.VMEM((128, PLANE * ROW), bf16),
                pltpu.VMEM((128, ROW), f32),
                pltpu.VMEM((1, ROW), f32),
                pltpu.SemaphoreType.DMA((6,)),
            ],
        ),
        out_shape=[jax.ShapeDtypeStruct((PACK + 32, 128), bf16)] * 2,
        compiler_params=pltpu.CompilerParams(vmem_limit_bytes=9 * 2**20),
        cost_estimate=pl.CostEstimate(flops=10 * 10**9, bytes_accessed=2**21, transcendentals=0),
        name="attend_forward",
    )(info, queries_a, queries_b, *keys_values, begin)


def combine_kernel(here, a_ref, b_ref, full_ref, log_ref, *out):
    logs = []
    for ref in (a_ref, b_ref):
        rows = ref[PACK:, :].astype(f32)
        logs.append(rows[:8] + rows[8:16] + rows[16:24])
    top = jnp.maximum(logs[0], logs[1])
    shares = [jnp.exp2(part - top) for part in logs]
    total = shares[0] + shares[1]
    log_ref[...] = top + jnp.log2(total)
    columns = [(share / total).T for share in shares]
    left = lax.broadcasted_iota(jnp.int32, (128, 128), 1) < 64
    for b in range(4):
        mixed = jnp.zeros((128, 128), f32)
        for ref, column in zip((a_ref, b_ref), columns):
            weight = jnp.where(left, column[:, 2 * b : 2 * b + 1], column[:, 2 * b + 1 : 2 * b + 2])
            mixed = mixed + weight * ref[128 * b : 128 * b + 128, :].astype(f32)
        full_ref[128 * b : 128 * b + 128, :] = mixed
        store_at(out, here[X], b, mixed.astype(bf16))


def combine(here, part_a, part_b):
    return run(
        combine_kernel,
        "combine",
        here,
        (part_a, part_b),
        [((PACK, 128), f32), ((8, 128), f32)] + [((128, 128), bf16)] * 4,
        megabytes=1, far=(0, 1),
    )


def grad_message_kernel(here, p0, p1, p2, p3, mixed_ref, log_ref, out_ref):
    for d, ref in enumerate((p0, p1, p2, p3)):
        out_ref[pl.ds(pl.multiple_of(before(here[X], d) * 128, 128), 128), :] = ref[...]
    deltas = []
    for b in range(4):
        rows = slice(128 * b, 128 * b + 128)
        each = (out_ref[rows, :].astype(f32) * mixed_ref[rows, :]).T
        deltas.append(jnp.sum(each[:64], axis=0, keepdims=True))
        deltas.append(jnp.sum(each[64:], axis=0, keepdims=True))
    parts = list(split_three(log_ref[...])) + list(split_three(jnp.concatenate(deltas, axis=0)))
    out_ref[PACK:, :] = jnp.concatenate(parts, axis=0).astype(bf16)


def grad_message(here, *operands):
    return run(grad_message_kernel, "grad_message", here, operands, [((PACK + 48, 128), bf16)], megabytes=1)[0]


def backward_kernel(
    info,
    qa,
    qb,
    ma,
    mb,
    kv0,
    kv1,
    kv2,
    kv3,
    begin_ref,
    dqa_ref,
    dqb_ref,
    own_ref,
    one_ref,
    two_ref,
    three_ref,
    qt_ref,
    gt_ref,
    q_ref,
    g_ref,
    kv_ref,
    kt_ref,
    row_ref,
    acc_ref,
    dq_acc,
    q_in,
    m_in,
    semaphores,
):
    tile = pl.program_id(0)

    def load(query_ref, message_ref):
        unpack_transposed(query_ref, qt_ref, 0)
        unpack_transposed(message_ref, gt_ref, 64)
        q_ref[...] = qt_ref[...].T
        g_ref[...] = gt_ref[...].T
        rows = message_ref[PACK:, :].astype(f32)
        for k in range(2):
            part = rows[24 * k : 24 * k + 8] + rows[24 * k + 8 : 24 * k + 16] + rows[24 * k + 16 : 24 * k + 24]
            for j in range(8):
                row_ref[k : k + 1, 128 * j : 128 * j + 128] = part[j : j + 1, :]

    @pl.when(tile == 0)
    def _():
        copies = [
            pltpu.make_async_copy(source, target, semaphores.at[k])
            for k, (source, target) in enumerate(
                [(qa, q_in.at[0]), (qb, q_in.at[1]), (ma, m_in.at[0]), (mb, m_in.at[1])]
                + plane_copies(info, (kv0, kv1, kv2, kv3), kv_ref)
            )
        ]
        for copy in copies:
            copy.start()
        acc_ref[...] = jnp.zeros(acc_ref.shape, f32)
        qt_ref[64:, :] = jnp.zeros((64, ROW), bf16)
        gt_ref[:64, :] = jnp.zeros((64, ROW), bf16)
        for copy in copies:
            copy.wait()
        for c in range(PLANE):
            kt_ref[:, c * ROW : c * ROW + ROW] = kv_ref[c * ROW : c * ROW + ROW, :].T

    load(q_in.at[tile], m_in.at[tile])
    dq_acc[...] = jnp.zeros(dq_acc.shape, f32)

    def step(c, masked):
        start = pl.multiple_of(c * ROW, ROW)
        block = kv_ref[pl.ds(start, ROW), :]
        scores = dot_nn(block, qt_ref[...]) * score_factor
        if masked:
            scores = jnp.where(visible(info, tile, c, begin_ref, scores.shape), scores, 2 * masked_score)
        weights = jnp.exp2(scores - row_ref[0:1, :])
        grad_weights = dot_nn(block, gt_ref[...])
        grad_scores = (weights * (grad_weights - row_ref[1:2, :])).astype(bf16)
        acc_ref[pl.ds(start, ROW), :] += dot_nn(grad_scores, q_ref[...]) + dot_nn(
            weights.astype(bf16), g_ref[...]
        )
        dq_acc[...] += dot_nn(kt_ref[:, pl.ds(start, ROW)], grad_scores)

    def body(c, carry):
        masked = needs_mask(info, tile, c)

        @pl.when(masked)
        def _():
            step(c, True)

        @pl.when(jnp.logical_not(masked))
        def _():
            step(c, False)

        return carry

    first, last = chunk_bounds(info, tile)
    lax.fori_loop(first, last, body, 0)

    @pl.when(tile == 0)
    def _():
        pack_transposed(dq_acc[:64, :], dqa_ref)

    @pl.when(tile == 1)
    def _():
        pack_transposed(dq_acc[:64, :], dqb_ref)
        for d, ref in enumerate((own_ref, one_ref, two_ref, three_ref)):
            start = pl.multiple_of(lax.rem(info[7] + d, 4) * ROW, ROW)
            ref[...] = acc_ref[pl.ds(start, ROW), :].astype(bf16)


def attend_backward(info, queries_a, queries_b, message_a, message_b, keys_values, begin):
    packed = pl.BlockSpec((PACK, 128), lambda i, s: (0, 0))
    hbm = pl.BlockSpec(memory_space=pltpu.HBM)
    block = pl.BlockSpec((ROW, 128), lambda i, s: (0, 0))
    return pl.pallas_call(
        backward_kernel,
        grid_spec=pltpu.PrefetchScalarGridSpec(
            num_scalar_prefetch=1,
            grid=(2,),
            in_specs=[hbm] * 8 + [pl.BlockSpec((1, ROW), lambda i, s: (0, i))],
            out_specs=[packed] * 2 + [block] * 4,
            scratch_shapes=[
                pltpu.VMEM((128, ROW), bf16),
                pltpu.VMEM((128, ROW), bf16),
                pltpu.VMEM((ROW, 128), bf16),
                pltpu.VMEM((ROW, 128), bf16),
                pltpu.VMEM((PLANE * ROW, 128), bf16),
                pltpu.VMEM((128, PLANE * ROW), bf16),
                pltpu.VMEM((8, ROW), f32),
                pltpu.VMEM((PLANE * ROW, 128), f32),
                pltpu.VMEM((128, ROW), f32),
                pltpu.VMEM((2, PACK, 128), bf16),
                pltpu.VMEM((2, PACK + 48, 128), bf16),
                pltpu.SemaphoreType.DMA((8,)),
            ],
        ),
        out_shape=[jax.ShapeDtypeStruct((PACK, 128), bf16)] * 2
        + [jax.ShapeDtypeStruct((ROW, 128), bf16)] * 4,
        compiler_params=pltpu.CompilerParams(vmem_limit_bytes=17 * 2**20),
        cost_estimate=pl.CostEstimate(flops=18 * 10**9, bytes_accessed=2**22, transcendentals=0),
        name="attend_backward",
    )(info, queries_a, queries_b, message_a, message_b, *keys_values, begin)


def inner_kernel(here, p0, p1, p2, p3, gain, weight, mixed_ref, mine, theirs, heads):
    for d, ref in enumerate((p0, p1, p2, p3)):
        heads[before(here[X], d)] = ref[...].astype(f32)
    mixed = jnp.concatenate([pair_unpack(heads[0], heads[1]), pair_unpack(heads[2], heads[3])], axis=1)
    mixed_ref[...] = mixed
    mean = jnp.mean(mixed, axis=-1, keepdims=True)
    centred = mixed - mean
    spread = jnp.sum(centred * centred, axis=-1, keepdims=True)
    projected = dot_nn((centred * gain[...]).astype(bf16), weight[...])
    for half in range(2):
        tokens = slice(128 * half, 128 * half + 128)
        stats = [row_of(mean[tokens]), row_of(spread[tokens])]
        slots = [jnp.where(here[PART] == j // 2, stats[j % 2], 0.0) for j in range(8)]
        row = jnp.broadcast_to(jnp.concatenate(slots, axis=1), (8, D))
        store_half(mine, theirs, here[CORE], half, jnp.concatenate([projected[tokens], row], axis=0))


def inner(here, *operands):
    return run(
        inner_kernel,
        "inner",
        here,
        operands,
        [((256, 256), f32), ((136, D), f32), ((136, D), f32)],
        [pltpu.VMEM((4, 128, 128), f32)],
        megabytes=3,
    )


def chip_stats_kernel(here, mine, other, out):
    total = mine[...] + other[...]
    high, middle, low = split_three(total[128:])
    index = lax.broadcasted_iota(jnp.int32, (8, D), 0)
    out[...] = jnp.concatenate([total[:128], jnp.where(index < 4, high, middle), low], axis=0).astype(bf16)


def join_stats_kernel(here, chip, far, out):
    total = chip[...].astype(f32) + far[...].astype(f32)
    row = total[128:129] + total[132:133] + total[136:137]
    out[...] = jnp.concatenate([total[:128], jnp.broadcast_to(row, (8, D))], axis=0)


def add_chip_kernel(here, mine, other, out):
    out[...] = (mine[...] + other[...]).astype(bf16)


def add_far_kernel(here, chip, far, out):
    out[...] = chip[...].astype(f32) + far[...].astype(f32)


def chip_stats(here, mine, other):
    return run(chip_stats_kernel, "chip_stats", here, (mine, other), [((144, D), bf16)], megabytes=1)[0]


def join_stats(here, chip, far):
    return run(join_stats_kernel, "join_stats", here, (chip, far), [((136, D), f32)], megabytes=1)[0]


def add_chip(here, mine, other):
    return run(add_chip_kernel, "add_chip", here, (mine, other), [((128, D), bf16)], megabytes=1)[0]


def add_far(here, chip, far):
    return run(add_far_kernel, "add_far", here, (chip, far), [((128, D), f32)], megabytes=1)[0]


def sum_ffn(here, mine, theirs):
    chip = add_chip(here, mine, core_swap(theirs))
    total = add_far(here, chip, far_swap(chip))
    return total, core_swap(total)


def gauss_share(values):
    return 0.5 + 0.5 * lax.erf(values * math.sqrt(0.5))


def feed_kernel(
    here,
    total,
    other,
    vectors,
    stream,
    vec,
    mixed_ref,
    weight,
    grad_hidden,
    both_ref,
    middle_ref,
    before_ref,
    unit_ref,
    inv_ref,
    sums_ref,
    halves,
):
    halves[here[CORE]] = total[...]
    halves[1 - here[CORE]] = other[...]
    ending = vectors[4:5, :] + vec[OUTPUT_BIAS : OUTPUT_BIAS + 1, :]
    inner_gain = vec[INNER : INNER + 1, :256]
    inner_bias = vec[INNER : INNER + 1, 256:512]
    for half in range(2):
        tokens = slice(128 * half, 128 * half + 128)
        stats = jnp.concatenate([halves[half, 128:129, 128 * j : 128 * j + 128] for j in range(8)], axis=0).T
        means = [stats[:, 2 * k : 2 * k + 1] for k in range(4)]
        mean = (means[0] + means[1] + means[2] + means[3]) * 0.25
        spread = stats[:, 1:2] + stats[:, 3:4] + stats[:, 5:6] + stats[:, 7:8]
        projected = halves[half, :128, :]
        for k in range(4):
            move = means[k] - mean
            spread = spread + 256.0 * move * move
            projected = projected + move * vectors[k : k + 1, :]
        inv = lax.rsqrt(spread / D + epsilon)
        middle_ref[tokens, :] = stream[tokens, :] + projected * inv + ending
        unit = (mixed_ref[tokens, :] - mean) * inv
        unit_ref[tokens, :] = unit
        inv_ref[tokens, :] = jnp.broadcast_to(inv, (128, 128))
        both_ref[tokens, D:] = (unit * inner_gain + inner_bias).astype(bf16)
    unit, _ = norm_parts(middle_ref[...])
    both_ref[:, :D] = (
        unit * vec[FEED_GAIN : FEED_GAIN + 1, :] + vec[FEED_BIAS : FEED_BIAS + 1, :]
    ).astype(bf16)
    before_act = dot_nn(both_ref[:, :D], weight[...]) + vec[UP_BIAS : UP_BIAS + 1, :]
    before_ref[...] = before_act
    active = before_act * gauss_share(before_act)
    scaled = grad_hidden[...] * vec[HIDDEN_GAIN : HIDDEN_GAIN + 1, :]
    columns = [
        jnp.sum(part, axis=-1, keepdims=True) for part in (active, active * active, scaled, scaled * active)
    ]
    lane = lax.broadcasted_iota(jnp.int32, (256, 128), 1)
    spread = jnp.zeros((256, 128), f32)
    for k, column in enumerate(columns):
        spread = jnp.where(lane == k, column, spread)
    sums_ref[...] = spread.T[:8]


def feed(here, *operands):
    return run(
        feed_kernel,
        "feed",
        here,
        operands,
        [
            ((256, D + 256), bf16),
            ((256, D), f32),
            ((256, D), f32),
            ((256, 256), f32),
            ((256, 128), f32),
            ((8, 256), f32),
        ],
        [pltpu.VMEM((2, 136, D), f32)],
        megabytes=10, far=(0, 1, 2, 3, 4),
    )


def hidden_kernel(
    here, sums, before_ref, grad_hidden, vec, weight, low_ref, small_ref, mine, theirs, o0, o1, o2, o3
):
    before_act = before_ref[...]
    share = gauss_share(before_act)
    slope = share + before_act * jnp.exp(-0.5 * before_act * before_act) * (1.0 / math.sqrt(2.0 * math.pi))
    columns = sums[...].T
    mean = columns[:, 0:1] / FF
    inv = lax.rsqrt(columns[:, 1:2] / FF - mean * mean + epsilon)
    first = columns[:, 2:3]
    cross = inv * (columns[:, 3:4] - mean * first)
    gain = vec[HIDDEN_GAIN : HIDDEN_GAIN + 1, :]
    unit = (before_act * share - mean) * inv
    low_ref[...] = (unit * gain + vec[HIDDEN_BIAS : HIDDEN_BIAS + 1, :]).astype(bf16)
    grad_out = grad_hidden[...]
    grad_pre = (inv * (grad_out * gain - first / FF - unit * (cross / FF)) * slope).astype(bf16)
    small_ref[0:1, :] = jnp.sum(grad_out * unit, axis=0, keepdims=True)
    small_ref[1:2, :] = jnp.sum(grad_out, axis=0, keepdims=True)
    small_ref[2:3, :] = jnp.sum(grad_pre.astype(f32), axis=0, keepdims=True)
    small_ref[3:, :] = jnp.zeros((5, D), f32)
    for k in range(4):
        lanes = slice(256 * k, 256 * k + 256)
        store_at((o0, o1, o2, o3), here[X], k, jnp.concatenate([low_ref[:, lanes], grad_pre[:, lanes]], axis=0))
    back = dot_nt(grad_pre, weight[...])
    for half in range(2):
        store_half(mine, theirs, here[CORE], half, back[128 * half : 128 * half + 128])


def hidden(here, *operands):
    return run(
        hidden_kernel,
        "hidden",
        here,
        operands,
        [((256, D), bf16), ((8, D), f32), ((128, D), f32), ((128, D), f32)] + [((512, 256), bf16)] * 4,
        megabytes=8, far=(1,),
    )


def feed_out_kernel(here, low_ref, weight, mine, theirs):
    for half in range(2):
        tokens = slice(128 * half, 128 * half + 128)
        store_half(mine, theirs, here[CORE], half, dot_nn(low_ref[tokens, :], weight[...]))


def feed_out(here, low, weight):
    return run(
        feed_out_kernel, "feed_out", here, (low, weight), [((128, D), f32), ((128, D), f32)], megabytes=2
    )


def result_kernel(here, total, other, middle, vec, out, halves):
    halves[here[CORE]] = total[...]
    halves[1 - here[CORE]] = other[...]
    for half in range(2):
        tokens = slice(128 * half, 128 * half + 128)
        out[tokens, :] = (
            middle[tokens, :] + halves[half] + vec[DOWN_BIAS : DOWN_BIAS + 1, :]
        ).astype(bf16)


def result_out(here, *operands):
    return run(
        result_kernel,
        "result",
        here,
        operands,
        [((256, D), bf16)],
        [pltpu.VMEM((2, 128, D), f32)],
        megabytes=4,
    )[0]


def feed_quarter_kernel(here, p0, p1, p2, p3, cotangent, both, out):
    down = jnp.zeros((256, D), f32)
    up = jnp.zeros((256, D), f32)
    for d, ref in enumerate((p0, p1, p2, p3)):
        tokens = pl.ds(pl.multiple_of(before(here[X], d) * 256, 256), 256)
        down = down + dot_tn(ref[:256, :], cotangent[tokens, :])
        up = up + dot_tn(ref[256:, :], both[tokens, :D])
    for y in range(4):
        for z in range(2):
            out[y, z, :128, :] = down[128 * z : 128 * z + 128, 256 * y : 256 * y + 256].astype(bf16)
            rows = slice(256 * y + 128 * z, 256 * y + 128 * z + 128)
            out[y, z, 128:, :] = up[:, rows].T.astype(bf16)


def feed_quarter(here, *operands):
    return run(
        feed_quarter_kernel, "feed_quarter", here, operands, [((4, 2, 256, 256), bf16)], megabytes=3
    )[0]


def middle_back_kernel(
    here,
    total,
    other,
    middle,
    stream,
    cotangent,
    vec,
    weight,
    unit_ref,
    inv_ref,
    vectors,
    grad_ref,
    small_ref,
    h0,
    h1,
    h2,
    h3,
    b0,
    b1,
    b2,
    b3,
    halves,
):
    halves[here[CORE]] = total[...]
    halves[1 - here[CORE]] = other[...]
    grad_feed = jnp.concatenate([halves[0], halves[1]], axis=0)
    unit, inv = norm_parts(middle[...])
    grad_result = cotangent[...].astype(f32)
    grad_middle = grad_result + norm_back(grad_feed, unit, inv, vec[FEED_GAIN : FEED_GAIN + 1, :])
    grad_ref[...] = grad_middle
    low = grad_middle.astype(bf16)
    branch = low.astype(f32)
    for k in range(4):
        store_at((b0, b1, b2, b3), here[X], k, low[:, 256 * k : 256 * k + 256])
    grad_inner = dot_nt(low, weight[...])
    through = vectors[0:1, :] + vectors[1:2, :] + vectors[2:3, :] + vectors[3:4, :]
    first = jnp.sum(branch * through, axis=-1, keepdims=True)
    ending = vectors[4:5, :] + vec[OUTPUT_BIAS : OUTPUT_BIAS + 1, :]
    cross = jnp.sum(branch * (middle[...] - stream[...] - ending), axis=-1, keepdims=True)
    inner_unit = unit_ref[...]
    inner_inv = inv_ref[:, 0:1]
    grad_mixed = inner_inv * (
        grad_inner * vec[INNER : INNER + 1, :256] - first / D - inner_unit * (cross / D)
    )
    for group in range(2):
        lanes = grad_mixed[:, 128 * group : 128 * group + 128]
        for side in range(2):
            store_at((h0, h1, h2, h3), here[X], 2 * group + side, pair_pack(lanes, side).astype(bf16))
    small_ref[0:1, :] = jnp.sum(grad_feed * unit, axis=0, keepdims=True)
    small_ref[1:2, :] = jnp.sum(grad_feed, axis=0, keepdims=True)
    small_ref[2:3, :] = jnp.sum(branch, axis=0, keepdims=True)
    small_ref[3:4, :] = jnp.sum(grad_result, axis=0, keepdims=True)
    small_ref[4:5, :256] = jnp.sum(grad_inner * inner_unit, axis=0, keepdims=True)
    small_ref[4:5, 256:512] = jnp.sum(grad_inner, axis=0, keepdims=True)
    small_ref[4:5, 512:] = jnp.zeros((1, 512), f32)
    small_ref[5:, :] = jnp.zeros((3, D), f32)


def middle_back(here, *operands):
    return run(
        middle_back_kernel,
        "middle_back",
        here,
        operands,
        [((256, D), f32), ((8, D), f32)] + [((128, 128), bf16)] * 4 + [((256, 256), bf16)] * 4,
        [pltpu.VMEM((2, 128, D), f32)],
        megabytes=10, far=(0, 1),
    )


def row_grads_kernel(
    here, own, one, two, three, qa, qb, kv_cos, kv_sin, q_cos, q_sin, out_ref, sums_ref, p0, p1, p2, p3
):
    def turned(values, cosine, sine):
        return (values * cosine + half_swapped(values) * sine).astype(bf16)

    for b in range(8):
        rows = slice(128 * b, 128 * b + 128)
        total = own[rows, :].astype(f32)
        for ref in (one, two, three):
            total = total + ref[rows, :].astype(f32)
        out_ref[rows, :128] = turned(total, kv_cos[rows, :], kv_sin[rows, :])
    for b in range(4):
        rows = slice(128 * b, 128 * b + 128)
        total = qa[rows, :].astype(f32) + qb[rows, :].astype(f32)
        for side in range(2):
            tokens = slice(256 * b + 128 * side, 256 * b + 128 * side + 128)
            values = total if side == 0 else pltpu.roll(total, 64, 1)
            out_ref[tokens, 128:] = turned(values, q_cos[tokens, :], q_sin[tokens, :])
    for b in range(4):
        store_at((p0, p1, p2, p3), here[X], b, out_ref[256 * b : 256 * b + 256, :])
    sums_ref[...] = jnp.broadcast_to(jnp.sum(out_ref[...].astype(f32), axis=0, keepdims=True), (8, 256))


def row_grads(here, *operands):
    return run(
        row_grads_kernel,
        "row_grads",
        here,
        operands,
        [((ROW, 256), bf16), ((8, 256), f32)] + [((256, 256), bf16)] * 4,
        megabytes=3,
    )


def head_weights_kernel(here, weight, out):
    left = lax.broadcasted_iota(jnp.int32, (256, 128), 1) < 64
    for r in range(4):
        rows = slice(256 * r, 256 * r + 256)
        for group in range(2):
            lanes = slice(128 * group, 128 * group + 128)
            query, key, value = [weight[s, rows, lanes].astype(f32) for s in range(3)]
            even = [jnp.where(left, key, pltpu.roll(value, 64, 1)), jnp.where(left, query, 0.0)]
            odd = [
                jnp.where(left, pltpu.roll(key, 64, 1), value),
                jnp.where(left, pltpu.roll(query, 64, 1), 0.0),
            ]
            for side, parts in enumerate((even, odd)):
                out[2 * group + side, rows, :] = jnp.concatenate(parts, axis=1).astype(bf16)


def head_weights(here, weight):
    return run(head_weights_kernel, "head_weights", here, (weight,), [((4, D, 256), bf16)], megabytes=2)[0]


def normed_back_kernel(here, p0, p1, p2, p3, weight, mine, theirs):
    for half in range(2):
        total = jnp.zeros((128, D), f32)
        for d, ref in enumerate((p0, p1, p2, p3)):
            total = total + dot_nt(ref[128 * half : 128 * half + 128, :], weight[before(here[X], d)])
        store_half(mine, theirs, here[CORE], half, total)


def normed_back(here, *operands):
    return run(
        normed_back_kernel, "normed_back", here, operands, [((128, D), f32), ((128, D), f32)], megabytes=2
    )


def attend_quarter_kernel(
    here, normed, projected, sums, both, s0, s1, s2, s3, small_a, small_b, q0, q1, q2, q3
):
    grad_input = dot_tn(projected[...], normed[...])
    grad_output = jnp.zeros((256, 256), f32)
    for d, ref in enumerate((s0, s1, s2, s3)):
        tokens = pl.ds(pl.multiple_of(before(here[X], d) * 256, 256), 256)
        grad_output = grad_output + dot_tn(both[tokens, D:], ref[...])
    slots = [jnp.where(here[X] == k, sums[0:1, :], 0.0) for k in range(4)]
    vectors = [small_a[k : k + 1, :] for k in range(3)] + [small_b[k : k + 1, :] for k in range(5)]
    left = lax.broadcasted_iota(jnp.int32, (128, 128), 1) < 64
    nothing = jnp.zeros((4, 256), f32)
    for y in range(4):
        parts = []
        group = grad_output[:, 128 * (y // 2) : 128 * (y // 2) + 128]
        for z in range(2):
            rows = slice(256 * y + 128 * z, 256 * y + 128 * z + 128)
            ours = group[128 * z : 128 * z + 128, :]
            ours = pltpu.roll(ours, 64, 1) if y % 2 == 0 else ours
            tall = grad_input[:, rows].T
            tall = jnp.concatenate([tall[:, :128], jnp.where(left, tall[:, 128:], ours)], axis=1)
            vector = vectors[2 * y + z]
            small = [vector[:, 256 * k : 256 * k + 256] for k in range(4)]
            small = small + (slots if y == 0 and z == 0 else [nothing]) + [nothing, nothing]
            parts.append(jnp.concatenate([tall] + small, axis=0).astype(bf16)[None])
        store_at((q0, q1, q2, q3), here[Y], y, jnp.concatenate(parts, axis=0))


def attend_quarter(here, *operands):
    return run(
        attend_quarter_kernel,
        "attend_quarter",
        here,
        operands,
        [((2, 144, 256), bf16)] * 4,
        megabytes=3,
    )


def add_four_kernel(here, p0, p1, p2, p3, out):
    total = p0[...].astype(f32) + p1[...].astype(f32) + p2[...].astype(f32) + p3[...].astype(f32)
    out[...] = total.astype(bf16)


def add_four(here, *pieces):
    return run(add_four_kernel, "add_four", here, pieces, [((2, 144, 256), bf16)], megabytes=1)[0]


def feed_weights_kernel(in_ref, down_ref, up_ref):
    for x in range(4):
        for z in range(2):
            rows = slice(256 * x + 128 * z, 256 * x + 128 * z + 128)
            down_ref[rows, :] = in_ref[0, x, z, :128, :].astype(f32)
            up_ref[128 * z : 128 * z + 128, 256 * x : 256 * x + 256] = in_ref[0, x, z, 128:, :].astype(f32)


def feed_weights_out(shared):
    return pl.pallas_call(
        feed_weights_kernel,
        grid=(4,),
        in_specs=[pl.BlockSpec((1, 4, 2, 256, 256), lambda y: (y, 0, 0, 0, 0))],
        out_specs=[pl.BlockSpec((D, 256), lambda y: (0, y)), pl.BlockSpec((256, D), lambda y: (y, 0))],
        out_shape=[jax.ShapeDtypeStruct((D, D), f32)] * 2,
        compiler_params=pltpu.CompilerParams(vmem_limit_bytes=6 * 2**20),
        name="feed_weights",
    )(shared)


def attend_weights_kernel(here, in_ref, input_ref, output_ref, *small_refs):
    for y in range(4):
        for z in range(2):
            rows = slice(256 * y + 128 * z, 256 * y + 128 * z + 128)
            blocks = [in_ref[y, x, z, :128, :].astype(f32) for x in range(4)]
            for s, start in enumerate((128, 0, 64)):
                input_ref[s, rows, :] = jnp.concatenate([b[:, start : start + 64] for b in blocks], axis=1)
            for x in range(4):
                output_ref[128 * z : 128 * z + 128, 256 * x + 64 * y : 256 * x + 64 * y + 64] = blocks[x][:, 192:]
            small = jnp.zeros((16, 256), f32)
            for x in range(4):
                small = small + in_ref[y, x, z, 128:, :].astype(f32)
            small_refs[2 * y + z][...] = jnp.concatenate([small[k : k + 1] for k in range(4)], axis=1)
            if y == 0 and z == 0:
                small_refs[8][...] = jnp.concatenate([small[k : k + 1] for k in range(4, 8)], axis=1)


def attend_weights_out(here, shared):
    return run(
        attend_weights_kernel,
        "attend_weights",
        here,
        (shared,),
        [((3, D, 256), f32), ((256, D), f32)] + [((1, D), f32)] * 9,
        megabytes=7,
    )


def leave_kernel(here, total, other, stream, grad_middle, vec, kind, out_ref, last_ref, halves):
    halves[here[CORE]] = total[...]
    halves[1 - here[CORE]] = other[...]
    grad_normed = jnp.concatenate([halves[0], halves[1]], axis=0)
    unit, inv = norm_parts(stream[...])
    grad = grad_middle[...] + norm_back(grad_normed, unit, inv, vec[ATTEND_GAIN : ATTEND_GAIN + 1, :])
    out_ref[...] = grad
    last_ref[0:1, :] = jnp.sum(grad_normed * unit, axis=0, keepdims=True)
    last_ref[1:2, :] = jnp.sum(grad_normed, axis=0, keepdims=True)
    for c in range(3):
        last_ref[2 + c : 3 + c, :] = jnp.sum(jnp.where(kind[...] == c, grad, 0.0), axis=0, keepdims=True)
    last_ref[5:, :] = jnp.zeros((3, D), f32)


def leave(here, *operands):
    return run(
        leave_kernel,
        "leave",
        here,
        operands,
        [((256, D), f32), ((8, D), f32)],
        [pltpu.VMEM((2, 128, D), f32)],
        megabytes=7,
    )


def ring_sum_kernel(axis, here, p0, p1, p2, p3, out, ring):
    for d, ref in enumerate((p0, p1, p2, p3)):
        ring[before(here[axis], d)] = ref[...]
    out[...] = ring[0] + ring[1] + ring[2] + ring[3]


def ring_sum(here, axis, *pieces):
    return run(
        partial(ring_sum_kernel, axis),
        "ring_sum",
        here,
        pieces,
        [((8, D), f32)],
        [pltpu.VMEM((4, 8, D), f32)],
        megabytes=1,
    )[0]


def last_sum_kernel(here, own, other, table_ref, gain_ref, bias_ref):
    total = own[...] + other[...]
    gain_ref[...] = total[0:1]
    bias_ref[...] = total[1:2]
    table_ref[...] = total[2:5]


def last_sum(here, own, other):
    return run(
        last_sum_kernel,
        "last_sum",
        here,
        (own, other),
        [((3, D), f32), ((1, D), f32), ((1, D), f32)],
        megabytes=1,
    )


ATTEND_GAIN, OUTPUT_BIAS, FEED_GAIN, FEED_BIAS, DOWN_BIAS, UP_BIAS, HIDDEN_GAIN, HIDDEN_BIAS, INNER = range(9)


def tables_of(positions, total_rows):
    pair_index = (jnp.arange(128) % 32).astype(f32)
    frequency = 1.0 / 10000.0 ** (pair_index / 32)
    angles = positions.astype(f32)[:, None] * frequency[None, :]
    ratios = (2.0 * pair_index + 0.4 * HEAD_DIM) / (1.4 * HEAD_DIM)
    exponent = (positions - total_rows // 2).astype(f32)[:, None] / scale_base
    return jnp.cos(angles), jnp.sin(angles), ratios[None, :] ** exponent


def back_tables(positions, total_rows, score_scale):
    lane = jnp.arange(128)
    cosine, sine, growth = tables_of(positions, total_rows)
    cosine = cosine * score_scale
    sine = sine * jnp.where(lane < 32, score_scale, -score_scale)[None]
    turned = (lane < 64)[None]
    return (
        jnp.where(turned, cosine / growth, 1.0),
        jnp.where(turned, sine / growth, 0.0),
        jnp.where(turned, cosine * growth, 0.0),
        jnp.where(turned, sine * growth, 0.0),
    )


def per_device(
    tokens,
    segment_kind,
    document,
    type_table,
    attend_gain,
    attend_bias,
    input_weight,
    input_bias,
    inner_gain,
    inner_bias,
    output_weight,
    output_bias,
    feed_gain,
    feed_bias,
    up_weight,
    up_bias,
    hidden_gain,
    hidden_bias,
    down_weight,
    down_bias,
    cotangent,
):
    local_rows = tokens.shape[0]
    total_rows = document.shape[0]
    local_width = input_weight.shape[2]
    score_scale = HEAD_DIM ** (-0.5)
    place = lax.axis_index("seq")
    part = lax.axis_index("ffn")
    y, z, x = place // 8, (place // 4) % 2, place % 4
    here = jnp.stack([x, y, z, part % 2, part, part, part, part]).astype(jnp.int32)
    query_pos = place * local_rows + jnp.arange(local_rows, dtype=jnp.int32)
    kind = segment_kind[:, None]

    stream, normed_low, *pieces = enter(
        here,
        tokens,
        kind,
        type_table,
        attend_gain[None],
        attend_bias[None],
        input_weight,
        input_bias,
        *tables_of(query_pos, total_rows),
    )
    received = shift_x(pieces)

    begins = jnp.zeros((total_rows,), jnp.int32)
    for number in range(1, 4):
        begins = begins + jnp.where(
            document >= number, jnp.sum((document == number - 1).astype(jnp.int32)), 0
        )
    row_a = jnp.where(y % 2 == z, y, 7 - y)
    row_b = 7 - row_a
    begin_a = lax.dynamic_slice_in_dim(begins, row_a * ROW, ROW)
    begin_b = lax.dynamic_slice_in_dim(begins, row_b * ROW, ROW)
    begin = jnp.concatenate([begin_a, begin_b])[None]
    info = jnp.stack([z, row_a, row_b, begin_a[0], begin_b[0], begin_a[-1], begin_b[-1], y]).astype(
        jnp.int32
    )
    row_kv, row_q = rows(here, pieces[0], *received)
    queries_a = lax.ppermute(row_q, "seq", TO_SAME)
    queries_b = lax.ppermute(row_q, "seq", TO_OTHER)
    kv_received = [lax.ppermute(row_kv, "seq", pairs) for pairs in Y_SHIFTS]
    cotangent_row = gather_x(after(cotangent, row_kv))
    normed_row = gather_x(after(normed_low, row_kv))
    output_weight_f = after(output_weight, row_kv).astype(f32)
    inner_gain_f = inner_gain.astype(f32)
    inner_bias_f = inner_bias.astype(f32)
    through = jnp.concatenate(
        [
            jnp.where(
                jnp.arange(4)[:, None] == part,
                jnp.sum(output_weight_f * inner_gain_f[:, None], axis=0)[None],
                0.0,
            ),
            jnp.sum(output_weight_f * inner_bias_f[:, None], axis=0)[None],
            jnp.zeros((3, D), f32),
        ],
        axis=0,
    )
    through = through + core_swap(through)
    through = through + far_swap(through)
    vec = jnp.concatenate(
        [
            v.astype(f32)
            for v in (
                attend_gain,
                output_bias,
                feed_gain,
                feed_bias,
                down_bias,
                up_bias,
                hidden_gain,
                hidden_bias,
                inner_gain,
                inner_bias,
            )
        ]
        + [jnp.zeros((16 * D - 8 * D - 512,), f32)]
    ).reshape(16, D)
    grad_hidden = jnp.einsum(
        "td,fd->tf", after(cotangent, row_kv), down_weight, preferred_element_type=f32
    )
    plane, queries_a, queries_b, through, vec, grad_hidden, begin, info = lax.optimization_barrier(
        ([row_kv] + kv_received, queries_a, queries_b, through, vec, grad_hidden, begin, info)
    )
    out_a, out_b = attend_forward(info, queries_a, queries_b, plane, begin)
    mixed_row, logs_row, *pieces = combine(
        here, lax.ppermute(out_a, "seq", FROM_SAME), lax.ppermute(out_b, "seq", FROM_OTHER)
    )
    mixed, mine, theirs = inner(
        here, pieces[0], *shift_x(pieces), inner_gain_f[None], output_weight
    )
    chip = chip_stats(here, mine, core_swap(theirs))
    total = join_stats(here, chip, far_swap(chip))
    both, middle, before_act, inner_unit, inner_inv, sums = feed(
        here, total, core_swap(total), through, stream, vec, mixed, up_weight, grad_hidden
    )
    both_row = gather_x(both)
    sums = sums + core_swap(sums)
    sums = sums + far_swap(sums)
    hidden_low, small_a, mine, theirs, *pieces = hidden(
        here, sums, before_act, grad_hidden, vec, up_weight
    )
    slices = shift_x(pieces)
    total, other = sum_ffn(here, mine, theirs)
    feed_mine, feed_theirs = feed_out(here, hidden_low, down_weight)
    feed_chip = add_chip(here, feed_mine, core_swap(feed_theirs))
    total, other, feed_chip = lax.optimization_barrier((total, other, feed_chip))
    slices = [pieces[0]] + slices
    grad_middle, small_b, *pieces = middle_back(
        here,
        total,
        other,
        middle,
        stream,
        cotangent,
        vec,
        output_weight,
        inner_unit,
        inner_inv,
        through,
    )
    head_pieces, branch_pieces = pieces[:4], pieces[4:]
    feed_quarters = feed_quarter(here, *slices, cotangent_row, both_row)
    head_received = shift_x(head_pieces)
    feed_far = far_swap(after(feed_chip, grad_middle))
    head_received, feed_quarters, feed_far = lax.optimization_barrier(
        (head_received, feed_quarters, feed_far)
    )
    message = grad_message(here, head_pieces[0], *head_received, mixed_row, logs_row)
    feed_sums = lax.psum_scatter(
        feed_quarters, "seq", scatter_dimension=0, axis_index_groups=Y_GROUPS
    )
    message_a = lax.ppermute(message, "seq", TO_SAME)
    message_b = lax.ppermute(message, "seq", TO_OTHER)
    branch_received = shift_x(branch_pieces)
    grad_qa, grad_qb, *kv_pieces = attend_backward(
        info, queries_a, queries_b, message_a, message_b, plane, begin
    )
    kv_pieces, feed_sums, branch_received = lax.optimization_barrier(
        (kv_pieces, feed_sums, branch_received)
    )
    kv_parts = shift_y(kv_pieces)
    q_parts = [lax.ppermute(grad_qa, "seq", FROM_SAME), lax.ppermute(grad_qb, "seq", FROM_OTHER)]
    feed_pairs = sum_z(feed_sums)
    feed_total = add_far(here, feed_chip, feed_far)
    result = result_out(here, feed_total, core_swap(feed_total), middle, vec)
    row_pos = (2 * y + z) * ROW + jnp.arange(ROW, dtype=jnp.int32)
    tables = back_tables(after(row_pos, kv_pieces[0]), total_rows, score_scale)
    weight_heads = head_weights(here, after(input_weight, kv_pieces[0]))
    kv_parts, q_parts, tables, feed_pairs, weight_heads, result = lax.optimization_barrier(
        (kv_parts, q_parts, tables, feed_pairs, weight_heads, result)
    )
    feed_shared = share_yx(feed_pairs)
    projected_row, projected_sums, *pieces = row_grads(here, kv_pieces[0], *kv_parts, *q_parts, *tables)
    back_received = shift_x(pieces)
    quarter_pieces = attend_quarter(
        here,
        normed_row,
        projected_row,
        projected_sums,
        both_row,
        branch_pieces[0],
        *branch_received,
        small_a,
        small_b,
    )
    back_received, quarter_pieces = lax.optimization_barrier((back_received, quarter_pieces))
    mine, theirs = normed_back(here, pieces[0], *back_received, weight_heads)
    quarter_received = shift_y(quarter_pieces)
    total, other = sum_ffn(here, mine, theirs)
    attend_pairs = sum_z(add_four(here, quarter_pieces[0], *quarter_received))
    total, other, attend_pairs, feed_shared = lax.optimization_barrier(
        (total, other, attend_pairs, feed_shared)
    )
    attend_shared = share_yx(attend_pairs)
    grad_tokens, last = leave(here, total, other, stream, grad_middle, vec, kind)
    last = ring_sum(here, X, last, *[lax.ppermute(last, "seq", pairs) for pairs in X_SHIFTS])
    last = ring_sum(here, Y, last, *[lax.ppermute(last, "seq", pairs) for pairs in Y_SHIFTS])
    grad_type_table, grad_attend_gain, grad_attend_bias = last_sum(
        here, last, lax.ppermute(last, "seq", Z_SWAP)
    )
    grad_down_weight, grad_up_weight = feed_weights_out(feed_shared)
    grad_input_weight, grad_output_weight, *small = attend_weights_out(here, attend_shared)
    small = [v.reshape(D) for v in small]
    input_sums = small[8].reshape(4, 4, HEAD_DIM)
    return (
        result,
        grad_tokens,
        grad_type_table,
        grad_attend_gain.reshape(D),
        grad_attend_bias.reshape(D),
        grad_input_weight,
        jnp.stack([input_sums[:, k].reshape(local_width) for k in (2, 0, 1)]),
        small[7][:local_width],
        small[7][local_width : 2 * local_width],
        grad_output_weight,
        small[5],
        small[3],
        small[4],
        grad_up_weight,
        small[2],
        small[0],
        small[1],
        grad_down_weight,
        small[6],
    )


def solution(mesh):
    in_specs = (
        P("seq", None),
        P("seq"),
        P(),
        P(),
        P(),
        P(),
        P(None, None, "ffn"),
        P(None, "ffn"),
        P("ffn"),
        P("ffn"),
        P("ffn", None),
        P(),
        P(),
        P(),
        P(None, "ffn"),
        P("ffn"),
        P("ffn"),
        P("ffn"),
        P("ffn", None),
        P(),
        P("seq", None),
    )
    out_specs = (
        P("seq", None),
        P("seq", None),
        P(),
        P(),
        P(),
        P(None, None, "ffn"),
        P(None, "ffn"),
        P("ffn"),
        P("ffn"),
        P("ffn", None),
        P(),
        P(),
        P(),
        P(None, "ffn"),
        P("ffn"),
        P("ffn"),
        P("ffn"),
        P("ffn", None),
        P(),
    )
    return jax.shard_map(
        per_device, mesh=mesh, in_specs=in_specs, out_specs=out_specs, check_vma=False
    )
```

time: 1400 us -> 364 us (0.26)
  waiting for transfers between devices: 958 us -> 103 us
  blocking collectives: 189 us -> 0 us
  matrix products: 102 us -> 2.34 us
  Pallas kernels: 0 us -> 94.5 us
  starting transfers between devices: 0.55 us -> 91.4 us
  local copies, waits for them, and re-layouts: 94.9 us -> 42.1 us
  other arithmetic: 35 us -> 12 us
    reduce_scatter x2 -> x1, waiting for transfers between devices: 349 us -> 0.02 us  [per_device(): lax.psum_scatter(feed_quarters, 'seq', scatter_dimension=0, axis_index_gr...]
    psum x4 -> x0, waiting for transfers between devices: 337 us -> none  [the longest x1 204 us: per_device(): summed = lax.psum(feed_grads + attention_grads, 'seq')]
    all_gather x2 -> x5, waiting for transfers between devices: 271 us -> 23.3 us  [the longest x2 23.3 us: share_yx(): values = lax.all_gather(values, 'seq', axis_index_groups=YX_GROUPS)]
    psum x5 -> x0, blocking collectives: 189 us -> none  [the longest x1 157 us: per_device(): summed = lax.psum(feed_grads + attention_grads, 'seq')]
    dot_general x62 -> x1, matrix products: 102 us -> 2.34 us  [per_device(): jnp.einsum('td,fd->tf', after(cotangent, row_kv), down_weight, preferred_...]
    pallas_call x0 -> x32, Pallas kernels: none -> 94.5 us  [the longest x29 59.3 us: run(): pl.pallas_call(body, in_specs=[pl.BlockSpec(memory_space=pltpu.SMEM)] + [...]
    ppermute x0 -> x60, starting transfers between devices: none -> 91.1 us  [the longest x18 34 us: shift_x(): lax.ppermute(piece, 'seq', pairs)]
    ppermute x0 -> x60, waiting for transfers between devices: none -> 78.9 us  [the longest x6 23.4 us: far_swap(): return lax.ppermute(values, 'ffn', FAR_SWAP)]
  transfers between devices with their start and end apart: 8 -> 66, of which waited for: 8 -> 29; matrix products, arithmetic and copies ran while one was open for 3% -> 4% of each run, Pallas kernels for 0% -> 24%
where the time goes in v1:
time: 364 us; the launch traced here: 361 us
  waiting for transfers between devices  103 us (28%)
  Pallas kernels  94.5 us (26%)
  starting transfers between devices  91.4 us (25%)
  local copies, waits for them, and re-layouts  42.1 us (12%)
  between operations  15.7 us (4%)
  other arithmetic  12 us (3%)
    pallas_call x29, Pallas kernels, run(): pl.pallas_call(body, in_specs=[pl.BlockSpec(memory_space=pltpu.SMEM)] + [...  59.3 us
    unnamed x174, local copies, waits for them, and re-layouts  35 us
    ppermute x18, starting transfers between devices, shift_x(): lax.ppermute(piece, 'seq', pairs)  34 us
    ppermute x6, waiting for transfers between devices, far_swap(): return lax.ppermute(values, 'ffn', FAR_SWAP)  23.4 us
    all_gather x2, waiting for transfers between devices, share_yx(): values = lax.all_gather(values, 'seq', axis_index_groups=YX_GROUPS)  23.3 us
    pallas_call x1, Pallas kernels, attend_backward(): pl.pallas_call(backward_kernel, grid_spec=pltpu.PrefetchScalarGridSpec(nu...  19.7 us
    ppermute x6, starting transfers between devices, shift_y(): lax.ppermute(piece, 'seq', pairs)  12.9 us
    pallas_call x1, Pallas kernels, attend_forward(): pl.pallas_call(forward_kernel, grid_spec=pltpu.PrefetchScalarGridSpec(num...  11.9 us
  transfers between devices with their start and end apart: 66, of which 29 were waited for; matrix products, arithmetic and copies ran while one was open for 4% of the time, Pallas kernels for 24%

profile of v1, /device:TPU:0, one launch (start us, length us, event | category | flops | bytes accessed | tf_op | source)
XLA Modules:
  0.0 360.9 jit_solution(15668332128856959730)
XLA Ops:
  14.4 3.2 enter.1
  19.2 2.7 collective-permute-start.1
  29.6 3.9 %collective-permute-start.9 = (f32[8,1024]{1,0:T(8,128)S(1)}, f32[8,1024]{1,0:T(8,128)}, u32[]{:S(2)}, u32[]{:S(2)}) collective-permute-start(f32[8,1024]{1,0:T(8,128)S(1)} %fusion.11), channel_id=1, source_target_pairs={{0,2},{1,3},{2,0},{3,1},{4,6},{5,7},{6,4},{7,5},{8,10},{9,11},{10,... | collective-permute-start | bytes 98312 | tf_op jit(solution)/shard_map/ppermute | solution.py:77
  33.5 2.7 stack.43.info
  37.8 2.9 collective-permute-start.4
  42.7 3.0 collective-permute-start.7
  45.7 2.3 fusion.16.refs_8_.refs_3_
  48.9 9.1 %collective-permute-done.7.qb = bf16[512,128]{1,0:T(8,128)(2,1)S(1)} collective-permute-done((bf16[512,128]{1,0:T(8,128)(2,1)S(1)}, bf16[512,128]{1,0:T(8,128)(2,1)S(1)}, u32[]{:S(2)}, u32[]{:S(2)}) %collective-permute-start.7) | collective-permute-done | bytes 131104 | tf_op jit(solution)/shard_map/ppermute | solution.py:1255
  58.1 11.9 %attend_forward.1 = (bf16[544,128]{1,0:T(8,128)(2,1)S(1)}, bf16[544,128]{1,0:T(8,128)(2,1)S(1)}) custom-call(s32[8]{0:T(128)S(1)} %stack.43.info, bf16[512,128]{1,0:T(8,128)(2,1)S(1)} %collective-permute-done.6.qa, bf16[512,128]{1,0:T(8,128)(2,1)S(1)} %collective-permute-done.7.qb, bf16[1024,128]{1,0:T(8,128)(2,1)} %get-tuple-element.167.kv0, ...), custom_call_target="tpu_custom_call" | custom-call | flops 10000000000 | bytes 2097152 | tf_op jit(solution)/shard_map/attend_forward/pallas_call | solution.py:410
  70.9 4.3 %collective-permute-start.11 = (bf16[544,128]{1,0:T(8,128)(2,1)S(1)}, bf16[544,128]{1,0:T(8,128)(2,1)S(1)}, u32[]{:S(2)}, u32[]{:S(2)}) collective-permute-start(bf16[544,128]{1,0:T(8,128)(2,1)S(1)} %get-tuple-element.173), channel_id=1, source_target_pairs={{16,0},{20,4},{24,8},{28,12},{32,16},{36,20},{40,24},{44,28},{80,3... | collective-permute-start | bytes 417800 | tf_op jit(solution)/shard_map/ppermute | solution.py:1302
  75.2 4.4 %collective-permute-done.11.refs_2_ = bf16[544,128]{1,0:T(8,128)(2,1)S(1)} collective-permute-done((bf16[544,128]{1,0:T(8,128)(2,1)S(1)}, bf16[544,128]{1,0:T(8,128)(2,1)S(1)}, u32[]{:S(2)}, u32[]{:S(2)}) %collective-permute-start.11) | collective-permute-done | bytes 139296 | tf_op jit(solution)/shard_map/ppermute | solution.py:1302
  79.6 14.0 %combine.1 = (f32[512,128]{1,0:T(8,128)S(1)}, f32[8,128]{1,0:T(8,128)S(1)}, bf16[128,128]{1,0:T(8,128)(2,1)S(1)}, bf16[128,128]{1,0:T(8,128)(2,1)S(1)}, bf16[128...) custom-call(s32[8]{0:T(128)S(1)} %stack.40.refs_0_, bf16[544,128]{1,0:T(8,128)(2,1)S(1)} %collective-permute-done.10.refs_1_, ...), custom_call_target="tpu_custom_call" | custom-call | flops 1048576 | bytes 675840 | tf_op jit(solution)/shard_map/combine/pallas_call | solution.py:125
  95.7 2.8 collective-permute-start.13
  107.2 9.8 %collective-permute-done.16.refs_2_ = bf16[144,1024]{1,0:T(8,128)(2,1)S(1)} collective-permute-done((bf16[144,1024]{1,0:T(8,128)(2,1)S(1)}, bf16[144,1024]{1,0:T(8,128)(2,1)S(1)}, u32[]{:S(2)}, u32[]{:S(2)}) %collective-permute-start.16) | collective-permute-done | bytes 294944 | tf_op jit(solution)/shard_map/ppermute | solution.py:77
  119.6 3.9 %feed.1 = (bf16[256,1280]{1,0:T(8,128)(2,1)S(1)}, f32[256,1024]{1,0:T(8,128)S(1)}, f32[256,1024]{1,0:T(8,128)S(1)}, f32[256,256]{1,0:T(8,128)S(1)}, f32[256,128]{1,0:T(8,128)S(1)}, /*index=5*/f32[8,256]{1,0:T(8,128)S(1)}) custom-call(s32[8]{0:T(128)S(1)} %stack.40.refs_0_, f32[136,1024]{1,0:T(8,128)S(1)} %join_stats.1.refs_1_, ...), custom_call_target="tpu_custom_call" | custom-call | flops 1048576 | bytes 8822784 | tf_op jit(solution)/shard_map/feed/pallas_call | solution.py:125
  129.7 4.4 %collective-permute-done.19 = f32[8,256]{1,0:T(8,128)S(1)} collective-permute-done((f32[8,256]{1,0:T(8,128)S(1)}, f32[8,256]{1,0:T(8,128)S(1)}, u32[]{:S(2)}, u32[]{:S(2)}) %collective-permute-start.19) | collective-permute-done | bytes 8224 | tf_op jit(solution)/shard_map/ppermute | solution.py:77
  137.0 3.0 hidden.1
  145.0 7.5 %collective-permute-done.21.refs_2_ = bf16[128,1024]{1,0:T(8,128)(2,1)S(1)} collective-permute-done((bf16[128,1024]{1,0:T(8,128)(2,1)S(1)}, bf16[128,1024]{1,0:T(8,128)(2,1)S(1)}, u32[]{:S(2)}, u32[]{:S(2)}) %collective-permute-start.21) | collective-permute-done | bytes 262176 | tf_op jit(solution)/shard_map/ppermute | solution.py:77
  153.6 3.6 collective-permute-start.28
  158.0 3.6 %middle_back.1 = (f32[256,1024]{1,0:T(8,128)S(1)}, f32[8,1024]{1,0:T(8,128)S(1)}, bf16[128,128]{1,0:T(8,128)(2,1)S(1)}, bf16[128,128]{1,0:T(8,128)(2,1)}, bf16[1...) custom-call(s32[8]{0:T(128)S(1)} %stack.40.refs_0_, ...), custom_call_target="tpu_custom_call" | custom-call | flops 1048576 | bytes 6422528 | tf_op jit(solution)/shard_map/middle_back/pallas_call | solution.py:125
  167.9 6.6 %collective-permute-start.25 = (bf16[128,128]{1,0:T(8,128)(2,1)}, bf16[128,128]{1,0:T(8,128)(2,1)S(1)}, u32[]{:S(2)}, u32[]{:S(2)}) collective-permute-start(bf16[128,128]{1,0:T(8,128)(2,1)} %get-tuple-element.199), channel_id=1, source_target_pairs={{0,8},{4,12},{8,0},{12,4},{16,24},{20,28},{24,16},{28,20},{32,40},... | collective-permute-start | bytes 98312 | tf_op jit(solution)/shard_map/ppermute | solution.py:65
  179.5 2.9 feed_quarter.1
  184.5 4.4 %collective-permute-start.32 = (bf16[560,128]{1,0:T(8,128)(2,1)S(1)}, bf16[560,128]{1,0:T(8,128)(2,1)S(1)}, u32[]{:S(2)}, u32[]{:S(2)}) collective-permute-start(bf16[560,128]{1,0:T(8,128)(2,1)S(1)} %grad_message.1), channel_id=1, source_target_pairs={{0,16},{4,20},{8,24},{12,28},{16,32},{20,36},{24,40},{28,44},{32,8... | collective-permute-start | bytes 430088 | tf_op jit(solution)/shard_map/ppermute | solution.py:1349
  191.0 2.7 collective-permute-start.35
  194.8 2.7 collective-permute-done.32.mb
  197.5 19.7 %attend_backward.1 = (bf16[512,128]{1,0:T(8,128)(2,1)}, bf16[512,128]{1,0:T(8,128)(2,1)}, bf16[1024,128]{1,0:T(8,128)(2,1)S(1)}, bf16[1024,128]{1,0:T(8,128)(2,1...) custom-call(s32[8]{0:T(128)S(1)} %copy-done.58, bf16[512,128]{1,0:T(8,128)(2,1)S(1)} %copy-done.66, ...), custom_call_target="tpu_custom_call" | custom-call | flops 17999998976 | bytes 4194304 | tf_op jit(solution)/shard_map/attend_backward/pallas_call | solution.py:593
  217.3 2.3 collective-permute-start.39
  221.3 5.0 %collective-permute-start.36 = (bf16[1024,128]{1,0:T(8,128)(2,1)}, bf16[1024,128]{1,0:T(8,128)(2,1)}, u32[]{:S(2)}, u32[]{:S(2)}) collective-permute-start(bf16[1024,128]{1,0:T(8,128)(2,1)} %get-tuple-element.222), channel_id=1, source_target_pairs={{0,32},{4,36},{8,40},{12,44},{16,48},{20,52},{24,56},{28,60},{32,6... | collective-permute-start | bytes 786440 | tf_op jit(solution)/shard_map/ppermute | solution.py:69
  226.8 2.1 collective-permute-start.38
  229.0 4.6 %fusion.7 = (f32[1024,128]{1,0:T(8,128)S(1)}, f32[1024,128]{1,0:T(8,128)}, f32[1024,128]{1,0:T(8,128)}, f32[1024,128]{1,0:T(8,128)}) fusion(f32[1024]{0:T(1024)S(1)} %get-tuple-element.311, f32[128]{0:T(128)S(1)} %compare_select_fusion, f32[128]{0:T(128)S(1)} %copy-done.77, f32[128]{0:T(128)S(1)} %copy-done.75, f32[1024]{0:T(1024)S(1)} %convert_element_type.118, ...), kind=kLoop, calls=%fused_computation.15 | loop fusion | flops 1441792 | bytes 2111104 | tf_op jit(solution)/shard_map/jit(_where)/select_n | solution.py:1189
  236.5 2.4 collective-permute-start.40
  239.6 2.1 collective-permute-done.40.refs_6_
  245.9 3.0 row_grads.1
  250.4 2.8 collective-permute-start.43
  253.3 2.7 collective-permute-start.45
  263.4 2.7 normed_back.1
  268.7 3.0 collective-permute-start.47
  271.9 5.0 %collective-permute-start.50 = (bf16[2,144,256]{2,1,0:T(8,128)(2,1)S(1)}, bf16[2,144,256]{2,1,0:T(8,128)(2,1)S(1)}, u32[]{:S(2)}, u32[]{:S(2)}) collective-permute-start(bf16[2,144,256]{2,1,0:T(8,128)(2,1)S(1)} %get-tuple-element.268), channel_id=1, source_target_pairs={{0,64},{4,68},{8,72},{12,76},{16,80},{20,84},{24,88},{28,92},{32,9... | collective-permute-start | bytes 442376 | tf_op jit(solution)/shard_map/ppermute | solution.py:69
  281.4 8.5 %collective-permute-done.50.refs_3_ = bf16[2,144,256]{2,1,0:T(8,128)(2,1)S(1)} collective-permute-done((bf16[2,144,256]{2,1,0:T(8,128)(2,1)S(1)}, bf16[2,144,256]{2,1,0:T(8,128)(2,1)S(1)}, u32[]{:S(2)}, u32[]{:S(2)}) %collective-permute-start.50) | collective-permute-done | bytes 147488 | tf_op jit(solution)/shard_map/ppermute | solution.py:69
  290.8 5.0 %collective-permute-done.52 = bf16[2,144,256]{2,1,0:T(8,128)(2,1)S(1)} collective-permute-done((bf16[2,144,256]{2,1,0:T(8,128)(2,1)S(1)}, bf16[2,144,256]{2,1,0:T(8,128)(2,1)S(1)}, u32[]{:S(2)}, u32[]{:S(2)}) %collective-permute-start.52) | collective-permute-done | bytes 147488 | tf_op jit(solution)/shard_map/ppermute | solution.py:90
  296.5 4.0 %all-gather.14.cloned.1.call-done = bf16[32,256,256]{2,1,0:T(8,128)(2,1)} async-done(((bf16[2,256,256]{2,1,0:T(8,128)(2,1)}), bf16[32,256,256]{2,1,0:T(8,128)(2,1)}) %all-gather.14.cloned.1.call-update) | async-done | bytes 4194320 | tf_op jit(solution)/shard_map/all_gather | solution.py:85
  300.5 2.6 leave.1
  303.1 2.9 collective-permute-start.54
  310.8 3.8 %collective-permute-start.57 = (f32[8,1024]{1,0:T(8,128)S(1)}, f32[8,1024]{1,0:T(8,128)S(1)}, u32[]{:S(2)}, u32[]{:S(2)}) collective-permute-start(f32[8,1024]{1,0:T(8,128)S(1)} %ring_sum.2.refs_1_), channel_id=1, source_target_pairs={{0,64},{4,68},{8,72},{12,76},{16,80},{20,84},{24,88},{28,92},{32,9... | collective-permute-start | bytes 98312 | tf_op jit(solution)/shard_map/ppermute | solution.py:1393
  319.9 2.2 copy-done.16
  322.1 3.5 feed_weights.1
  326.8 19.3 %all-gather.16.cloned.1.call-done = bf16[32,144,256]{2,1,0:T(8,128)(2,1)} async-done(((bf16[2,144,256]{2,1,0:T(8,128)(2,1)}), bf16[32,144,256]{2,1,0:T(8,128)(2,1)}) %all-gather.16.cloned.1.call-update) | async-done | bytes 2359312 | tf_op jit(solution)/shard_map/all_gather | solution.py:85
  347.8 3.3 attend_weights.1
  (353 shorter events, 110.5 us)
Async XLA Ops:
  7.3 167.8 %all-gather.8.cloned.1.call-start = ((), (), s32[]{:S(2)}) async-start(), calls=%async_computation.1 | async-start | bytes 2621440 | tf_op jit(solution)/shard_map/all_gather | solution.py:81
  17.6 8.8 %collective-permute-start = (bf16[384,128]{1,0:T(8,128)(2,1)S(1)}, bf16[384,128]{1,0:T(8,128)(2,1)S(1)}, u32[]{:S(2)}, u32[]{:S(2)}) collective-permute-start(bf16[384,128]{1,0:T(8,128)(2,1)S(1)} %get-tuple-element.157), channel_id=1, source_target_pairs={{0,4},{4,8},{8,12},{12,0},{16,20},{20,24},{24,28},{28,16},{32,36},... | collective-permute-start | bytes 294920 | tf_op jit(solution)/shard_map/ppermute | solution.py:65
  19.2 7.3 %collective-permute-start.1 = (bf16[384,128]{1,0:T(8,128)(2,1)S(1)}, bf16[384,128]{1,0:T(8,128)(2,1)S(1)}, u32[]{:S(2)}, u32[]{:S(2)}) collective-permute-start(bf16[384,128]{1,0:T(8,128)(2,1)S(1)} %get-tuple-element.158), channel_id=1, source_target_pairs={{0,8},{4,12},{8,0},{12,4},{16,24},{20,28},{24,16},{28,20},{32,40},... | collective-permute-start | bytes 294920 | tf_op jit(solution)/shard_map/ppermute | solution.py:65
  28.9 146.3 %all-gather.10.cloned.1.call-start = ((), (), s32[]{:S(2)}) async-start(), calls=%async_computation.2 | async-start | bytes 3276800 | tf_op jit(solution)/shard_map/all_gather | solution.py:81
  29.6 13.2 %collective-permute-start.9 = (f32[8,1024]{1,0:T(8,128)S(1)}, f32[8,1024]{1,0:T(8,128)}, u32[]{:S(2)}, u32[]{:S(2)}) collective-permute-start(f32[8,1024]{1,0:T(8,128)S(1)} %fusion.11), channel_id=1, source_target_pairs={{0,2},{1,3},{2,0},{3,1},{4,6},{5,7},{6,4},{7,5},{8,10},{9,11},{10,... | collective-permute-start | bytes 98312 | tf_op jit(solution)/shard_map/ppermute | solution.py:77
  36.2 21.8 %collective-permute-start.3 = (bf16[1024,128]{1,0:T(8,128)(2,1)}, bf16[1024,128]{1,0:T(8,128)(2,1)S(1)}, u32[]{:S(2)}, u32[]{:S(2)}) collective-permute-start(bf16[1024,128]{1,0:T(8,128)(2,1)} %get-tuple-element.167.kv0), channel_id=1, source_target_pairs={{0,32},{4,36},{8,40},{12,44},{16,48},{20,52},{24,56},{28,60},{32,6... | collective-permute-start | bytes 786440 | tf_op jit(solution)/shard_map/ppermute | solution.py:1256
  37.8 20.2 %collective-permute-start.4 = (bf16[1024,128]{1,0:T(8,128)(2,1)}, bf16[1024,128]{1,0:T(8,128)(2,1)S(1)}, u32[]{:S(2)}, u32[]{:S(2)}) collective-permute-start(bf16[1024,128]{1,0:T(8,128)(2,1)} %get-tuple-element.167.kv0), channel_id=1, source_target_pairs={{0,64},{4,68},{8,72},{12,76},{16,80},{20,84},{24,88},{28,92},{32,9... | collective-permute-start | bytes 786440 | tf_op jit(solution)/shard_map/ppermute | solution.py:1256
  40.7 17.3 %collective-permute-start.5 = (bf16[1024,128]{1,0:T(8,128)(2,1)}, bf16[1024,128]{1,0:T(8,128)(2,1)S(1)}, u32[]{:S(2)}, u32[]{:S(2)}) collective-permute-start(bf16[1024,128]{1,0:T(8,128)(2,1)} %get-tuple-element.167.kv0), channel_id=1, source_target_pairs={{0,96},{4,100},{8,104},{12,108},{16,112},{20,116},{24,120},{28,124... | collective-permute-start | bytes 786440 | tf_op jit(solution)/shard_map/ppermute | solution.py:1256
  42.0 6.8 %collective-permute-start.6 = (bf16[512,128]{1,0:T(8,128)(2,1)S(1)}, bf16[512,128]{1,0:T(8,128)(2,1)S(1)}, u32[]{:S(2)}, u32[]{:S(2)}) collective-permute-start(bf16[512,128]{1,0:T(8,128)(2,1)S(1)} %get-tuple-element.161), channel_id=1, source_target_pairs={{0,0},{4,4},{8,8},{12,12},{16,48},{20,52},{24,56},{28,60},{32,64},... | collective-permute-start | bytes 393224 | tf_op jit(solution)/shard_map/ppermute | solution.py:1254
  42.7 15.3 %collective-permute-start.7 = (bf16[512,128]{1,0:T(8,128)(2,1)S(1)}, bf16[512,128]{1,0:T(8,128)(2,1)S(1)}, u32[]{:S(2)}, u32[]{:S(2)}) collective-permute-start(bf16[512,128]{1,0:T(8,128)(2,1)S(1)} %get-tuple-element.161), channel_id=1, source_target_pairs={{0,16},{4,20},{8,24},{12,28},{16,32},{20,36},{24,40},{28,44},{32,8... | collective-permute-start | bytes 393224 | tf_op jit(solution)/shard_map/ppermute | solution.py:1255
  70.9 8.7 %collective-permute-start.11 = (bf16[544,128]{1,0:T(8,128)(2,1)S(1)}, bf16[544,128]{1,0:T(8,128)(2,1)S(1)}, u32[]{:S(2)}, u32[]{:S(2)}) collective-permute-start(bf16[544,128]{1,0:T(8,128)(2,1)S(1)} %get-tuple-element.173), channel_id=1, source_target_pairs={{16,0},{20,4},{24,8},{28,12},{32,16},{36,20},{40,24},{44,28},{80,3... | collective-permute-start | bytes 417800 | tf_op jit(solution)/shard_map/ppermute | solution.py:1302
  106.3 10.6 %collective-permute-start.16 = (bf16[144,1024]{1,0:T(8,128)(2,1)S(1)}, bf16[144,1024]{1,0:T(8,128)(2,1)S(1)}, u32[]{:S(2)}, u32[]{:S(2)}) collective-permute-start(bf16[144,1024]{1,0:T(8,128)(2,1)S(1)} %chip_stats.1.refs_1_), channel_id=1, source_target_pairs={{0,2},{1,3},{2,0},{3,1},{4,6},{5,7},{6,4},{7,5},{8,10},{9,11},{10,... | collective-permute-start | bytes 884744 | tf_op jit(solution)/shard_map/ppermute | solution.py:77
  127.6 93.6 %reduce-scatter.2.cloned.1.call-start = ((), (), s32[]{:S(2)}) async-start(), calls=%async_computation.3 | async-start | bytes 1310720 | tf_op jit(solution)/shard_map/reduce_scatter | solution.py:1345
  142.6 9.9 %collective-permute-start.21 = (bf16[128,1024]{1,0:T(8,128)(2,1)S(1)}, bf16[128,1024]{1,0:T(8,128)(2,1)S(1)}, u32[]{:S(2)}, u32[]{:S(2)}) collective-permute-start(bf16[128,1024]{1,0:T(8,128)(2,1)S(1)} %add_chip.3.refs_1_), channel_id=1, source_target_pairs={{0,2},{1,3},{2,0},{3,1},{4,6},{5,7},{6,4},{7,5},{8,10},{9,11},{10,... | collective-permute-start | bytes 786440 | tf_op jit(solution)/shard_map/ppermute | solution.py:77
  144.9 12.4 %collective-permute-start.23 = (f32[128,1024]{1,0:T(8,128)S(1)}, f32[128,1024]{1,0:T(8,128)S(1)}, u32[]{:S(2)}, u32[]{:S(2)}) collective-permute-start(f32[128,1024]{1,0:T(8,128)S(1)} %get-tuple-element.191), channel_id=1, source_target_pairs={{0,1},{1,0},{2,3},{3,2},{4,5},{5,4},{6,7},{7,6},{8,9},{9,8},{10,11... | collective-permute-start | bytes 1572872 | tf_op jit(solution)/shard_map/ppermute | solution.py:73
  153.2 14.7 %collective-permute-start.27 = (bf16[512,256]{1,0:T(8,128)(2,1)S(1)}, bf16[512,256]{1,0:T(8,128)(2,1)S(1)}, u32[]{:S(2)}, u32[]{:S(2)}) collective-permute-start(bf16[512,256]{1,0:T(8,128)(2,1)S(1)} %get-tuple-element.202), channel_id=1, source_target_pairs={{0,4},{4,8},{8,12},{12,0},{16,20},{20,24},{24,28},{28,16},{32,36},... | collective-permute-start | bytes 786440 | tf_op jit(solution)/shard_map/ppermute | solution.py:65
  153.6 20.8 %collective-permute-start.28 = (bf16[512,256]{1,0:T(8,128)(2,1)S(1)}, bf16[512,256]{1,0:T(8,128)(2,1)S(1)}, u32[]{:S(2)}, u32[]{:S(2)}) collective-permute-start(bf16[512,256]{1,0:T(8,128)(2,1)S(1)} %get-tuple-element.203), channel_id=1, source_target_pairs={{0,8},{4,12},{8,0},{12,4},{16,24},{20,28},{24,16},{28,20},{32,40},... | collective-permute-start | bytes 786440 | tf_op jit(solution)/shard_map/ppermute | solution.py:65
  157.2 17.3 %collective-permute-start.29 = (bf16[512,256]{1,0:T(8,128)(2,1)S(1)}, bf16[512,256]{1,0:T(8,128)(2,1)S(1)}, u32[]{:S(2)}, u32[]{:S(2)}) collective-permute-start(bf16[512,256]{1,0:T(8,128)(2,1)S(1)} %get-tuple-element.204), channel_id=1, source_target_pairs={{0,12},{4,0},{8,4},{12,8},{16,28},{20,16},{24,20},{28,24},{32,44},... | collective-permute-start | bytes 786440 | tf_op jit(solution)/shard_map/ppermute | solution.py:65
  163.8 18.6 %collective-permute-start.30 = (bf16[128,1024]{1,0:T(8,128)(2,1)S(1)}, bf16[128,1024]{1,0:T(8,128)(2,1)S(1)}, u32[]{:S(2)}, u32[]{:S(2)}) collective-permute-start(bf16[128,1024]{1,0:T(8,128)(2,1)S(1)} %add_chip.4.refs_1_), channel_id=1, source_target_pairs={{0,2},{1,3},{2,0},{3,1},{4,6},{5,7},{6,4},{7,5},{8,10},{9,11},{10,... | collective-permute-start | bytes 786440 | tf_op jit(solution)/shard_map/ppermute | solution.py:77
  164.6 17.8 %collective-permute-start.24 = (bf16[128,128]{1,0:T(8,128)(2,1)}, bf16[128,128]{1,0:T(8,128)(2,1)S(1)}, u32[]{:S(2)}, u32[]{:S(2)}) collective-permute-start(bf16[128,128]{1,0:T(8,128)(2,1)} %get-tuple-element.198), channel_id=1, source_target_pairs={{0,4},{4,8},{8,12},{12,0},{16,20},{20,24},{24,28},{28,16},{32,36},... | collective-permute-start | bytes 98312 | tf_op jit(solution)/shard_map/ppermute | solution.py:65
  167.9 14.5 %collective-permute-start.25 = (bf16[128,128]{1,0:T(8,128)(2,1)}, bf16[128,128]{1,0:T(8,128)(2,1)S(1)}, u32[]{:S(2)}, u32[]{:S(2)}) collective-permute-start(bf16[128,128]{1,0:T(8,128)(2,1)} %get-tuple-element.199), channel_id=1, source_target_pairs={{0,8},{4,12},{8,0},{12,4},{16,24},{20,28},{24,16},{28,20},{32,40},... | collective-permute-start | bytes 98312 | tf_op jit(solution)/shard_map/ppermute | solution.py:65
  174.4 8.0 %collective-permute-start.26 = (bf16[128,128]{1,0:T(8,128)(2,1)}, bf16[128,128]{1,0:T(8,128)(2,1)S(1)}, u32[]{:S(2)}, u32[]{:S(2)}) collective-permute-start(bf16[128,128]{1,0:T(8,128)(2,1)} %get-tuple-element.200), channel_id=1, source_target_pairs={{0,12},{4,0},{8,4},{12,8},{16,28},{20,16},{24,20},{28,24},{32,44},... | collective-permute-start | bytes 98312 | tf_op jit(solution)/shard_map/ppermute | solution.py:65
  182.4 73.6 %all-gather.12.cloned.1.call-start = ((), (), s32[]{:S(2)}) async-start(), calls=%async_computation.4 | async-start | bytes 2621440 | tf_op jit(solution)/shard_map/all_gather | solution.py:81
  183.0 117.4 %all-gather.14.cloned.1.call-start = ((), (), s32[]{:S(2)}) async-start(), calls=%async_computation.5 | async-start | bytes 4456448 | tf_op jit(solution)/shard_map/all_gather | solution.py:85
  183.8 10.4 %collective-permute-start.31 = (bf16[560,128]{1,0:T(8,128)(2,1)S(1)}, bf16[560,128]{1,0:T(8,128)(2,1)S(1)}, u32[]{:S(2)}, u32[]{:S(2)}) collective-permute-start(bf16[560,128]{1,0:T(8,128)(2,1)S(1)} %grad_message.1), channel_id=1, source_target_pairs={{0,0},{4,4},{8,8},{12,12},{16,48},{20,52},{24,56},{28,60},{32,64},... | collective-permute-start | bytes 430088 | tf_op jit(solution)/shard_map/ppermute | solution.py:1348
  184.5 13.0 %collective-permute-start.32 = (bf16[560,128]{1,0:T(8,128)(2,1)S(1)}, bf16[560,128]{1,0:T(8,128)(2,1)S(1)}, u32[]{:S(2)}, u32[]{:S(2)}) collective-permute-start(bf16[560,128]{1,0:T(8,128)(2,1)S(1)} %grad_message.1), channel_id=1, source_target_pairs={{0,16},{4,20},{8,24},{12,28},{16,32},{20,36},{24,40},{28,44},{32,8... | collective-permute-start | bytes 430088 | tf_op jit(solution)/shard_map/ppermute | solution.py:1349
  188.9 32.3 %collective-permute-start.33 = (bf16[256,256]{1,0:T(8,128)(2,1)}, bf16[256,256]{1,0:T(8,128)(2,1)S(1)}, u32[]{:S(2)}, u32[]{:S(2)}) collective-permute-start(bf16[256,256]{1,0:T(8,128)(2,1)} %get-tuple-element.219), channel_id=1, source_target_pairs={{0,4},{4,8},{8,12},{12,0},{16,20},{20,24},{24,28},{28,16},{32,36},... | collective-permute-start | bytes 393224 | tf_op jit(solution)/shard_map/ppermute | solution.py:65
  190.9 30.3 %collective-permute-start.34 = (bf16[256,256]{1,0:T(8,128)(2,1)}, bf16[256,256]{1,0:T(8,128)(2,1)S(1)}, u32[]{:S(2)}, u32[]{:S(2)}) collective-permute-start(bf16[256,256]{1,0:T(8,128)(2,1)} %get-tuple-element.220), channel_id=1, source_target_pairs={{0,8},{4,12},{8,0},{12,4},{16,24},{20,28},{24,16},{28,20},{32,40},... | collective-permute-start | bytes 393224 | tf_op jit(solution)/shard_map/ppermute | solution.py:65
  191.0 30.2 %collective-permute-start.35 = (bf16[256,256]{1,0:T(8,128)(2,1)}, bf16[256,256]{1,0:T(8,128)(2,1)S(1)}, u32[]{:S(2)}, u32[]{:S(2)}) collective-permute-start(bf16[256,256]{1,0:T(8,128)(2,1)} %get-tuple-element.221), channel_id=1, source_target_pairs={{0,12},{4,0},{8,4},{12,8},{16,28},{20,16},{24,20},{28,24},{32,44},... | collective-permute-start | bytes 393224 | tf_op jit(solution)/shard_map/ppermute | solution.py:65
  194.3 25.3 %collective-permute-start.42 = (f32[128,1024]{1,0:T(8,128)S(1)}, f32[128,1024]{1,0:T(8,128)S(1)}, u32[]{:S(2)}, u32[]{:S(2)}) collective-permute-start(f32[128,1024]{1,0:T(8,128)S(1)} %add_far.4.refs_1_), channel_id=1, source_target_pairs={{0,1},{1,0},{2,3},{3,2},{4,5},{5,4},{6,7},{7,6},{8,9},{9,8},{10,11... | collective-permute-start | bytes 1572872 | tf_op jit(solution)/shard_map/ppermute | solution.py:73
  217.3 22.4 %collective-permute-start.39 = (bf16[512,128]{1,0:T(8,128)(2,1)}, bf16[512,128]{1,0:T(8,128)(2,1)}, u32[]{:S(2)}, u32[]{:S(2)}) collective-permute-start(bf16[512,128]{1,0:T(8,128)(2,1)} %get-tuple-element.225), channel_id=1, source_target_pairs={{0,0},{4,4},{8,8},{12,12},{48,16},{52,20},{56,24},{60,28},{64,32},... | collective-permute-start | bytes 393224 | tf_op jit(solution)/shard_map/ppermute | solution.py:1358
  221.3 20.5 %collective-permute-start.36 = (bf16[1024,128]{1,0:T(8,128)(2,1)}, bf16[1024,128]{1,0:T(8,128)(2,1)}, u32[]{:S(2)}, u32[]{:S(2)}) collective-permute-start(bf16[1024,128]{1,0:T(8,128)(2,1)} %get-tuple-element.222), channel_id=1, source_target_pairs={{0,32},{4,36},{8,40},{12,44},{16,48},{20,52},{24,56},{28,60},{32,6... | collective-permute-start | bytes 786440 | tf_op jit(solution)/shard_map/ppermute | solution.py:69
  226.2 15.6 %collective-permute-start.37 = (bf16[1024,128]{1,0:T(8,128)(2,1)}, bf16[1024,128]{1,0:T(8,128)(2,1)}, u32[]{:S(2)}, u32[]{:S(2)}) collective-permute-start(bf16[1024,128]{1,0:T(8,128)(2,1)} %get-tuple-element.223), channel_id=1, source_target_pairs={{0,64},{4,68},{8,72},{12,76},{16,80},{20,84},{24,88},{28,92},{32,9... | collective-permute-start | bytes 786440 | tf_op jit(solution)/shard_map/ppermute | solution.py:69
  226.8 15.0 %collective-permute-start.38 = (bf16[1024,128]{1,0:T(8,128)(2,1)}, bf16[1024,128]{1,0:T(8,128)(2,1)}, u32[]{:S(2)}, u32[]{:S(2)}) collective-permute-start(bf16[1024,128]{1,0:T(8,128)(2,1)} %get-tuple-element.224), channel_id=1, source_target_pairs={{0,96},{4,100},{8,104},{12,108},{16,112},{20,116},{24,120},{28,124... | collective-permute-start | bytes 786440 | tf_op jit(solution)/shard_map/ppermute | solution.py:69
  229.0 7.5 %collective-permute-start.41 = (bf16[2,256,256]{2,1,0:T(8,128)(2,1)}, bf16[2,256,256]{2,1,0:T(8,128)(2,1)S(1)}, u32[]{:S(2)}, u32[]{:S(2)}) collective-permute-start(bf16[2,256,256]{2,1,0:T(8,128)(2,1)} %bitcast.32), channel_id=1, source_target_pairs={{0,16},{4,20},{8,24},{12,28},{16,0},{20,4},{24,8},{28,12},{32,48},... | collective-permute-start | bytes 786440 | tf_op jit(solution)/shard_map/ppermute | solution.py:90
  241.8 104.3 %all-gather.16.cloned.1.call-start = ((), (), s32[]{:S(2)}) async-start(), calls=%async_computation.6 | async-start | bytes 2506752 | tf_op jit(solution)/shard_map/all_gather | solution.py:85
  250.4 13.0 %collective-permute-start.43 = (bf16[256,256]{1,0:T(8,128)(2,1)}, bf16[256,256]{1,0:T(8,128)(2,1)}, u32[]{:S(2)}, u32[]{:S(2)}) collective-permute-start(bf16[256,256]{1,0:T(8,128)(2,1)} %get-tuple-element.243), channel_id=1, source_target_pairs={{0,4},{4,8},{8,12},{12,0},{16,20},{20,24},{24,28},{28,16},{32,36},... | collective-permute-start | bytes 393224 | tf_op jit(solution)/shard_map/ppermute | solution.py:65
  253.2 10.2 %collective-permute-start.44 = (bf16[256,256]{1,0:T(8,128)(2,1)}, bf16[256,256]{1,0:T(8,128)(2,1)}, u32[]{:S(2)}, u32[]{:S(2)}) collective-permute-start(bf16[256,256]{1,0:T(8,128)(2,1)} %get-tuple-element.244), channel_id=1, source_target_pairs={{0,8},{4,12},{8,0},{12,4},{16,24},{20,28},{24,16},{28,20},{32,40},... | collective-permute-start | bytes 393224 | tf_op jit(solution)/shard_map/ppermute | solution.py:65
  253.3 10.1 %collective-permute-start.45 = (bf16[256,256]{1,0:T(8,128)(2,1)}, bf16[256,256]{1,0:T(8,128)(2,1)}, u32[]{:S(2)}, u32[]{:S(2)}) collective-permute-start(bf16[256,256]{1,0:T(8,128)(2,1)} %get-tuple-element.245), channel_id=1, source_target_pairs={{0,12},{4,0},{8,4},{12,8},{16,28},{20,16},{24,20},{28,24},{32,44},... | collective-permute-start | bytes 393224 | tf_op jit(solution)/shard_map/ppermute | solution.py:65
  268.7 9.9 %collective-permute-start.47 = (bf16[128,1024]{1,0:T(8,128)(2,1)S(1)}, bf16[128,1024]{1,0:T(8,128)(2,1)S(1)}, u32[]{:S(2)}, u32[]{:S(2)}) collective-permute-start(bf16[128,1024]{1,0:T(8,128)(2,1)S(1)} %add_chip.5.refs_1_), channel_id=1, source_target_pairs={{0,2},{1,3},{2,0},{3,1},{4,6},{5,7},{6,4},{7,5},{8,10},{9,11},{10,... | collective-permute-start | bytes 786440 | tf_op jit(solution)/shard_map/ppermute | solution.py:77
  271.8 9.6 %collective-permute-start.49 = (bf16[2,144,256]{2,1,0:T(8,128)(2,1)S(1)}, bf16[2,144,256]{2,1,0:T(8,128)(2,1)S(1)}, u32[]{:S(2)}, u32[]{:S(2)}) collective-permute-start(bf16[2,144,256]{2,1,0:T(8,128)(2,1)S(1)} %get-tuple-element.267), channel_id=1, source_target_pairs={{0,32},{4,36},{8,40},{12,44},{16,48},{20,52},{24,56},{28,60},{32,6... | collective-permute-start | bytes 442376 | tf_op jit(solution)/shard_map/ppermute | solution.py:69
  271.9 18.0 %collective-permute-start.50 = (bf16[2,144,256]{2,1,0:T(8,128)(2,1)S(1)}, bf16[2,144,256]{2,1,0:T(8,128)(2,1)S(1)}, u32[]{:S(2)}, u32[]{:S(2)}) collective-permute-start(bf16[2,144,256]{2,1,0:T(8,128)(2,1)S(1)} %get-tuple-element.268), channel_id=1, source_target_pairs={{0,64},{4,68},{8,72},{12,76},{16,80},{20,84},{24,88},{28,92},{32,9... | collective-permute-start | bytes 442376 | tf_op jit(solution)/shard_map/ppermute | solution.py:69
  276.9 13.0 %collective-permute-start.51 = (bf16[2,144,256]{2,1,0:T(8,128)(2,1)S(1)}, bf16[2,144,256]{2,1,0:T(8,128)(2,1)S(1)}, u32[]{:S(2)}, u32[]{:S(2)}) collective-permute-start(bf16[2,144,256]{2,1,0:T(8,128)(2,1)S(1)} %get-tuple-element.269), channel_id=1, source_target_pairs={{0,96},{4,100},{8,104},{12,108},{16,112},{20,116},{24,120},{28,124... | collective-permute-start | bytes 442376 | tf_op jit(solution)/shard_map/ppermute | solution.py:69
  279.3 17.2 %collective-permute-start.48 = (f32[128,1024]{1,0:T(8,128)S(1)}, f32[128,1024]{1,0:T(8,128)S(1)}, u32[]{:S(2)}, u32[]{:S(2)}) collective-permute-start(f32[128,1024]{1,0:T(8,128)S(1)} %add_far.5.refs_1_), channel_id=1, source_target_pairs={{0,1},{1,0},{2,3},{3,2},{4,5},{5,4},{6,7},{7,6},{8,9},{9,8},{10,11... | collective-permute-start | bytes 1572872 | tf_op jit(solution)/shard_map/ppermute | solution.py:73
  303.1 5.5 %collective-permute-start.53 = (f32[8,1024]{1,0:T(8,128)S(1)}, f32[8,1024]{1,0:T(8,128)S(1)}, u32[]{:S(2)}, u32[]{:S(2)}) collective-permute-start(f32[8,1024]{1,0:T(8,128)S(1)} %get-tuple-element.274.refs_1_), channel_id=1, source_target_pairs={{0,4},{4,8},{8,12},{12,0},{16,20},{20,24},{24,28},{28,16},{32,36},... | collective-permute-start | bytes 98312 | tf_op jit(solution)/shard_map/ppermute | solution.py:1392
  303.1 5.5 %collective-permute-start.54 = (f32[8,1024]{1,0:T(8,128)S(1)}, f32[8,1024]{1,0:T(8,128)S(1)}, u32[]{:S(2)}, u32[]{:S(2)}) collective-permute-start(f32[8,1024]{1,0:T(8,128)S(1)} %get-tuple-element.274.refs_1_), channel_id=1, source_target_pairs={{0,8},{4,12},{8,0},{12,4},{16,24},{20,28},{24,16},{28,20},{32,40},... | collective-permute-start | bytes 98312 | tf_op jit(solution)/shard_map/ppermute | solution.py:1392
  310.8 6.1 %collective-permute-start.57 = (f32[8,1024]{1,0:T(8,128)S(1)}, f32[8,1024]{1,0:T(8,128)S(1)}, u32[]{:S(2)}, u32[]{:S(2)}) collective-permute-start(f32[8,1024]{1,0:T(8,128)S(1)} %ring_sum.2.refs_1_), channel_id=1, source_target_pairs={{0,64},{4,68},{8,72},{12,76},{16,80},{20,84},{24,88},{28,92},{32,9... | collective-permute-start | bytes 98312 | tf_op jit(solution)/shard_map/ppermute | solution.py:1393
  319.4 6.2 %collective-permute-start.59 = (f32[8,1024]{1,0:T(8,128)S(1)}, f32[8,1024]{1,0:T(8,128)S(1)}, u32[]{:S(2)}, u32[]{:S(2)}) collective-permute-start(f32[8,1024]{1,0:T(8,128)S(1)} %ring_sum.3.refs_1_), channel_id=1, source_target_pairs={{0,16},{4,20},{8,24},{12,28},{16,0},{20,4},{24,8},{28,12},{32,48},... | collective-permute-start | bytes 98312 | tf_op jit(solution)/shard_map/ppermute | solution.py:1395
  (105 other events, 1056.1 us)
Sparse Core Ops, SparseCore 0:
  29.0 32.9 all-gather.7
  127.8 39.6 all-gather.9
  182.6 23.4 reduce-scatter.1
  208.3 30.8 all-gather.11
  241.9 58.4 all-gather.13
  303.2 42.8 all-gather.15
